TPU v7x, 32 devices: a whole 2x2x4 slice. The times are simulated.
32 devices in a mesh: dp: 4 (over z), seq: 8 (over y, x, core).
Axes of the slice: x: 2, y: 2, z: 4, core: 2. Of those that a mesh axis runs over, the one named last changes fastest.
Arguments:
- tokens: bfloat16 [4096, 2688], P(('dp', 'seq')), may hold values from -6 to 6
- q_weight: bfloat16 [2688, 4096], P('dp', 'seq'), may hold values from -0.125 to 0.125
- key_projection: bfloat16 [2688, 2048], P('dp', 'seq'), may hold values from -0.125 to 0.125
- value_projection: bfloat16 [2688, 2048], P('dp', 'seq'), may hold values from -0.125 to 0.125
- query_norm_gain: float32 [128], replicated, may hold values from 0.5 to 2.5
- key_norm_gain: float32 [128], replicated, may hold values from 0.5 to 2.5
- doc_lengths: int32 [4, 4], P('dp'), may hold values from 1 to 768, 1024 in all within a row
- out_cot: bfloat16 [4096, 4096], P('dp', 'seq'), may hold values from -6 to 6
Outputs:
- attn_out: bfloat16 [4096, 4096], P(('dp', 'seq'))
- token_grad: bfloat16 [4096, 2688], P(('dp', 'seq'))
- q_weight_grad: float32 [2688, 4096], P('dp', 'seq')
- k_weight_grad: float32 [2688, 2048], P('dp', 'seq')
- v_weight_grad: float32 [2688, 2048], P('dp', 'seq')
Inputs may be any that keep to these rules, and one draw needn't show every extreme that they name: `doc_lengths`: each row's 4 lengths add up to 1024, and in every row the longest document has exactly 768 tokens.
All inputs are finite; a program needn't handle non-finite values.
Results may differ from a plain program's by a relative error of at most 0.015.
Values may be sent and summed in bfloat16 or wider, within the bound.
No kernel may reach another device: no remote copies, remote signals or barrier semaphores. Data moves between devices by JAX's collectives and lax.ppermute only.
A program may use at most 128 MiB of HBM per device.

v0:
```python
import functools

import jax
import jax.numpy as jnp
from jax import lax
from jax.experimental import pallas as pl
from jax.experimental.pallas import tpu as pltpu
from jax.sharding import PartitionSpec as P

HEAD_WIDTH = 128
WINDOW = 1024
QUERY_BLOCK = 256

score_scale = 168.0 ** (-0.5)
rope_base = 10000.0
log2_e = 1.4426950408889634
norm_eps = 1e-06
NN = (((1,), (0,)), ((), ()))
NT = (((1,), (1,)), ((), ()))
TN = (((0,), (0,)), ((), ()))


def dot(a, b, dims):
    return lax.dot_general(a, b, dims, preferred_element_type=jnp.float32)


def doc_tables(length_row, length):
    ends = jnp.cumsum(length_row, dtype=jnp.int32)
    starts = ends - length_row
    token = jnp.arange(length, dtype=jnp.int32)
    inside = (token[:, None] >= starts[None, :]) & (token[:, None] < ends[None, :])
    start = jnp.sum(jnp.where(inside, starts[None, :], 0), axis=1, dtype=jnp.int32)
    half = HEAD_WIDTH // 2
    inverse = rope_base ** (-jnp.arange(half, dtype=jnp.float32) * (2.0 / HEAD_WIDTH))
    angle = (token - start).astype(jnp.float32)[:, None] * inverse[None, :]
    cosine, sine = jnp.cos(angle), jnp.sin(angle)
    return (
        jnp.concatenate([cosine, cosine], axis=1),
        jnp.concatenate([-sine, sine], axis=1),
    )


def rotate(vectors, gain, cosine, sine):
    factor = lax.rsqrt(jnp.mean(vectors * vectors, axis=1, keepdims=True) + norm_eps)
    normed = vectors * factor * gain
    return normed * cosine + pltpu.roll(normed, HEAD_WIDTH // 2, 1) * sine


def rotate_back(grad, vectors, gain, cosine, sine):
    factor = lax.rsqrt(jnp.mean(vectors * vectors, axis=1, keepdims=True) + norm_eps)
    inner = (grad * cosine + pltpu.roll(grad * sine, HEAD_WIDTH // 2, 1)) * gain
    shared = jnp.mean(inner * vectors, axis=1, keepdims=True) * (factor * factor * factor)
    return inner * factor - vectors * shared


def first_keys(lengths_ref, query_token):
    first, end = jnp.maximum(query_token - (WINDOW - 1), 0), 0
    for document in range(lengths_ref.shape[1]):
        end = end + lengths_ref[0, document]
        first = jnp.maximum(first, jnp.where(query_token >= end, end, 0))
    return first


def head_kernel(share, halves, spots, marks, lengths_ref, qgain_ref, kgain_ref, *refs):
    count = len(spots)
    pieces = refs[:count]
    tokens_hbm, cos_hbm, sin_hbm, cot_hbm = refs[count : count + 4]
    refs = refs[count + 4 + marks :]
    out_ref, grad_ref, weight_hbm, terms_hbm = refs[:4]
    (tok, weight, cos_ref, sin_ref, cot_ref, proj, query, key, value, key_sum, value_sum, terms) = refs[4:16]
    piece_sem, tok_sem, small_sem, weight_sem, terms_sem = refs[16:]
    length, rows = tok.shape[0], pieces[0].shape[0]
    part_width = weight.shape[1] // halves
    blocks = length // QUERY_BLOCK
    mine = lax.axis_index("dp")

    def each_piece(act):
        for index, planes in enumerate(spots):
            half = index * halves // count
            cols = pl.ds(half * part_width, part_width)
            place = functools.reduce(
                lambda other, spot: jnp.where(mine == spot[0], spot[1], other), planes, 0
            )
            here = functools.reduce(
                lambda other, spot: other | (mine == spot[0]), planes[1:], mine == planes[0][0]
            )

            @pl.when(here)
            def _():
                at = pl.ds(pl.multiple_of(place * rows, 16), rows)
                act(pltpu.make_async_copy(pieces[index], weight.at[at, cols], piece_sem.at[index]))

    def tok_copy(block):
        at = pl.ds(pl.multiple_of(block * QUERY_BLOCK, QUERY_BLOCK), QUERY_BLOCK)
        return pltpu.make_async_copy(tokens_hbm.at[at], tok.at[at], tok_sem.at[block])

    small = [
        pltpu.make_async_copy(source, target, small_sem.at[slot])
        for slot, (source, target) in enumerate(
            ((cos_hbm, cos_ref), (sin_hbm, sin_ref), (cot_hbm, cot_ref))
        )
    ]
    each_piece(lambda copy: copy.start())
    for block in range(blocks):
        tok_copy(block).start()
    for copy in small:
        copy.start()
    each_piece(lambda copy: copy.wait())
    weight_copy = pltpu.make_async_copy(weight, weight_hbm, weight_sem)
    weight_copy.start()

    qgain, kgain = qgain_ref[...], kgain_ref[...]
    key_at, value_at = share * HEAD_WIDTH, (share + 1) * HEAD_WIDTH
    for copy in small:
        copy.wait()

    @pl.loop(0, blocks)
    def _(block):
        tok_copy(block).wait()
        at = pl.ds(pl.multiple_of(block * QUERY_BLOCK, QUERY_BLOCK), QUERY_BLOCK)
        part = dot(tok[at, :], weight[...], NN)
        proj[at, :] = part
        cosine, sine = cos_ref[at, :], sin_ref[at, :]
        for head in range(share):
            cols = slice(head * HEAD_WIDTH, (head + 1) * HEAD_WIDTH)
            query[at, cols] = rotate(part[:, cols], qgain, cosine, sine).astype(jnp.bfloat16)
        key[at, :] = rotate(part[:, key_at:value_at], kgain, cosine, sine).astype(jnp.bfloat16)
        value[at, :] = part[:, value_at:].astype(jnp.bfloat16)

    key_sum[...] = jnp.zeros_like(key_sum)
    value_sum[...] = jnp.zeros_like(value_sum)
    for block in range(blocks):
        start = block * QUERY_BLOCK
        low = max(0, (start - (WINDOW - 1)) // QUERY_BLOCK * QUERY_BLOCK)
        width = start + QUERY_BLOCK - low
        at, keys_at = pl.ds(start, QUERY_BLOCK), pl.ds(low, width)
        key_token = low + lax.broadcasted_iota(jnp.int32, (QUERY_BLOCK, width), 1)
        query_token = start + lax.broadcasted_iota(jnp.int32, (QUERY_BLOCK, 1), 0)
        allowed = (key_token >= first_keys(lengths_ref, query_token)) & (key_token <= query_token)
        key_part, value_part = key[keys_at, :], value[keys_at, :]
        cosine, sine = cos_ref[at, :], sin_ref[at, :]
        for head in range(share):
            cols = slice(head * HEAD_WIDTH, (head + 1) * HEAD_WIDTH)
            query_part, cot_part = query[at, cols], cot_ref[at, cols]
            scores = dot(query_part, key_part, NT) * (score_scale * log2_e)
            weights = jnp.where(allowed, jnp.exp2(scores), 0.0)
            probs = weights * (1.0 / jnp.sum(weights, axis=1, keepdims=True))
            probs_bf = probs.astype(jnp.bfloat16)
            mixed = dot(probs_bf, value_part, NN)
            out_ref[at, cols] = mixed.astype(jnp.bfloat16)
            value_sum[keys_at, :] += dot(probs_bf, cot_part, TN)
            grad_probs = dot(cot_part, value_part, NT)
            delta = jnp.sum(mixed * cot_part.astype(jnp.float32), axis=1, keepdims=True)
            grad_scores = (probs * (grad_probs - delta)).astype(jnp.bfloat16)
            key_sum[keys_at, :] += dot(grad_scores, query_part, TN)
            grad_query = dot(grad_scores, key_part, NN) * score_scale
            grad_ref[at, cols] = rotate_back(
                grad_query, proj[at, cols], qgain, cosine, sine
            ).astype(jnp.bfloat16)
    for block in range(blocks):
        at = pl.ds(block * QUERY_BLOCK, QUERY_BLOCK)
        grad_ref[at, key_at:value_at] = rotate_back(
            key_sum[at, :] * score_scale,
            proj[at, key_at:value_at],
            kgain,
            cos_ref[at, :],
            sin_ref[at, :],
        ).astype(jnp.bfloat16)
        grad_ref[at, value_at:] = value_sum[at, :].astype(jnp.bfloat16)

    grads = grad_ref[...]
    model = tok.shape[1]
    depth = model // terms_sem.shape[0]

    def terms_copy(part):
        at = pl.ds(pl.multiple_of(part * depth, HEAD_WIDTH), depth)
        return pltpu.make_async_copy(terms.at[at], terms_hbm.at[at], terms_sem.at[part])

    @pl.loop(0, terms_sem.shape[0])
    def _(part):
        at = pl.ds(pl.multiple_of(part * depth, HEAD_WIDTH), depth)
        terms[at, :] = dot(tok[:, at], grads, TN).astype(jnp.bfloat16)
        terms_copy(part).start()

    @pl.loop(0, terms_sem.shape[0])
    def _(part):
        terms_copy(part).wait()

    weight_copy.wait()


def heads(share, halves, pieces, spots, row_tokens, tables, gains, lengths, cot, marks):
    length, model = row_tokens.shape
    width = pieces[0].shape[1] * halves
    blocks = length // QUERY_BLOCK
    parts = max(k for k in (1, 3, 7) if model % (k * HEAD_WIDTH) == 0)
    hbm = pl.BlockSpec(memory_space=pltpu.HBM)
    vmem = pl.BlockSpec(memory_space=pltpu.VMEM)
    table = pltpu.VMEM((length, HEAD_WIDTH), jnp.float32)
    return pl.pallas_call(
        functools.partial(head_kernel, share, halves, spots, len(marks)),
        out_shape=(
            jax.ShapeDtypeStruct((length, share * HEAD_WIDTH), jnp.bfloat16),
            jax.ShapeDtypeStruct((length, width), jnp.bfloat16),
            jax.ShapeDtypeStruct((model, width), jnp.bfloat16),
            jax.ShapeDtypeStruct((model, width), jnp.bfloat16),
        ),
        in_specs=[pl.BlockSpec(memory_space=pltpu.SMEM), vmem, vmem]
        + [hbm] * (len(pieces) + 4 + len(marks)),
        out_specs=(vmem, vmem, hbm, hbm),
        scratch_shapes=[
            pltpu.VMEM((length, model), jnp.bfloat16),
            pltpu.VMEM((model, width), jnp.bfloat16),
            table,
            table,
            pltpu.VMEM((length, share * HEAD_WIDTH), jnp.bfloat16),
            pltpu.VMEM((length, width), jnp.float32),
            pltpu.VMEM((length, share * HEAD_WIDTH), jnp.bfloat16),
            pltpu.VMEM((length, HEAD_WIDTH), jnp.bfloat16),
            pltpu.VMEM((length, HEAD_WIDTH), jnp.bfloat16),
            table,
            table,
            pltpu.VMEM((model, width), jnp.bfloat16),
            pltpu.SemaphoreType.DMA((len(pieces),)),
            pltpu.SemaphoreType.DMA((blocks,)),
            pltpu.SemaphoreType.DMA((3,)),
            pltpu.SemaphoreType.DMA,
            pltpu.SemaphoreType.DMA((parts,)),
        ],
        compiler_params=pltpu.CompilerParams(vmem_limit_bytes=65024 * 1024),
        cost_estimate=pl.CostEstimate(
            flops=4 * length * model * width + 12 * share * length * length * HEAD_WIDTH,
            bytes_accessed=2 * (length * model + 3 * model * width + 4 * length * width),
            transcendentals=share * length * length,
        ),
        name="heads",
    )(lengths, *gains, *pieces, row_tokens, *tables, cot, *marks)


def token_kernel(adds, parts, marks, side_ref, grad_ref, weight_ref, *refs):
    grad = grad_ref[...]
    batch, rows = grad.shape[:2]
    grad = grad.reshape(batch * rows, grad.shape[2])
    total = dot(grad, weight_ref[...], NT).reshape(batch, rows, weight_ref.shape[0])
    for index in range(adds):
        total = total + refs[index][...].astype(jnp.float32)
    pieces, outs = refs[adds : adds + parts], refs[adds + parts + marks :]
    if not parts and len(outs) == 1:
        outs[0][...] = total.astype(jnp.bfloat16)
        return
    count = parts or len(outs)
    for place in range(count):

        @pl.when(pl.program_id(0) == place // batch)
        def _():
            row = total[place % batch]
            if parts:
                row = row + pieces[place][...].astype(jnp.float32)
                outs[0][place % batch] = row.astype(jnp.bfloat16)
            else:
                outs[place][...] = row.astype(jnp.bfloat16)


def token_terms(grad, weight, side, owners, adds, parts, marks, split):
    length, width = grad.shape
    model = weight.shape[0]
    rows, pairs = length // owners, owners // 2
    batch = 2 if pairs % 2 == 0 else 1
    block = pl.BlockSpec((batch, rows, model), lambda i, side_ref: (i, 0, 0))
    single = pl.BlockSpec((rows, model), lambda i, side_ref: (0, 0))
    out_specs, out_shape = block, jax.ShapeDtypeStruct((pairs, rows, model), jnp.bfloat16)
    if split:
        out_specs = (single,) * pairs
        out_shape = (jax.ShapeDtypeStruct((rows, model), jnp.bfloat16),) * pairs
    return pl.pallas_call(
        functools.partial(token_kernel, len(adds), len(parts), len(marks)),
        grid_spec=pltpu.PrefetchScalarGridSpec(
            num_scalar_prefetch=1,
            grid=(pairs // batch,),
            in_specs=[
                pl.BlockSpec(
                    (batch, None, rows, width), lambda i, side_ref: (i, side_ref[0], 0, 0)
                ),
                pl.BlockSpec((model, width), lambda i, side_ref: (0, 0)),
            ]
            + [block] * len(adds)
            + [single] * len(parts)
            + [pl.BlockSpec(memory_space=pltpu.HBM)] * len(marks),
            out_specs=out_specs,
        ),
        out_shape=out_shape,
        compiler_params=pltpu.CompilerParams(vmem_limit_bytes=65024 * 1024),
        cost_estimate=pl.CostEstimate(
            flops=length * width, bytes_accessed=length * width, transcendentals=0
        ),
        name="token_terms",
    )(side.reshape(1), grad.reshape(pairs, 2, rows, width), weight, *adds, *parts, *marks)


def mix_kernel(outs, count, marks, *refs):
    sources, refs = refs[:count], refs[count + marks :]
    targets, extra, sem = refs[: len(outs)], refs[len(outs) : -1], refs[-1]
    mine = lax.axis_index("dp")

    def each(act):
        for index, cases in enumerate(outs):
            for low, high, terms in cases:
                copies = []

                @pl.when((mine >= low) & (mine < high))
                def _():
                    for slot, (source, place) in enumerate(terms):
                        ref = sources[source]
                        ref = ref if place is None else ref.at[mine + place]
                        target = targets[index] if slot == 0 else extra[index]
                        copies.append(pltpu.make_async_copy(ref, target, sem.at[index, slot]))
                    act(index, copies)

    def start(index, copies):
        for copy in copies:
            copy.start()

    def finish(index, copies):
        for copy in copies:
            copy.wait()
        if len(copies) > 1:
            total = targets[index][...].astype(jnp.float32) + extra[index][...].astype(jnp.float32)
            targets[index][...] = total.astype(jnp.bfloat16)

    each(start)
    each(finish)


def mix(outs, sources, marks):
    shape = sources[0].shape[-2:]
    plain = pl.BlockSpec(memory_space=pl.ANY)
    vmem = pl.BlockSpec(memory_space=pltpu.VMEM)
    return pl.pallas_call(
        functools.partial(mix_kernel, outs, len(sources), len(marks)),
        out_shape=(jax.ShapeDtypeStruct(shape, jnp.bfloat16),) * len(outs),
        in_specs=[plain] * (len(sources) + len(marks)),
        out_specs=(vmem,) * len(outs),
        scratch_shapes=[pltpu.VMEM(shape, jnp.bfloat16)] * len(outs)
        + [pltpu.SemaphoreType.DMA((len(outs), 2))],
        compiler_params=pltpu.CompilerParams(vmem_limit_bytes=65024 * 1024),
        cost_estimate=pl.CostEstimate(flops=1, bytes_accessed=1, transcendentals=0),
        name="mix",
    )(*sources, *marks)


def scatter_cases(planes, step, terms, received_up, received_down):
    first, last = planes - step, step - planes
    ups = [(0, 1, [(terms, first)]), (1, step, [(terms, first), (received_up, None)])]
    downs = [
        (planes - 1, planes, [(terms, last)]),
        (planes - step, planes - 1, [(terms, last), (received_down, None)]),
    ]
    return ups, downs


def total_kernel(share, layout, count, *refs):
    sources, outs, pieces, sem = refs[:count], refs[count : count + 3], refs[count + 3 : -1], refs[-1]
    mine = lax.axis_index("dp")

    def each(act):
        for index, cases in enumerate(layout):
            for low, high, source, own in cases:

                @pl.when((mine >= low) & (mine < high))
                def _():
                    ref = sources[source].at[mine] if own else sources[source]
                    act(pltpu.make_async_copy(ref, pieces[index], sem.at[index]))

    each(lambda copy: copy.start())
    each(lambda copy: copy.wait())
    wide = share * HEAD_WIDTH
    for group in range(len(layout) // 3):
        total = sum(pieces[3 * group + index][...].astype(jnp.float32) for index in range(3))
        outs[0][:, group * wide : (group + 1) * wide] = total[:, :wide]
        narrow = slice(group * HEAD_WIDTH, (group + 1) * HEAD_WIDTH)
        outs[1][:, narrow] = total[:, wide : wide + HEAD_WIDTH]
        outs[2][:, narrow] = total[:, wide + HEAD_WIDTH :]


def total_terms(share, layout, sources):
    groups = len(layout) // 3
    rows, width = sources[0].shape[-2:]
    plain = pl.BlockSpec(memory_space=pl.ANY)
    vmem = pl.BlockSpec(memory_space=pltpu.VMEM)
    return pl.pallas_call(
        functools.partial(total_kernel, share, layout, len(sources)),
        out_shape=tuple(
            jax.ShapeDtypeStruct((rows, groups * count * HEAD_WIDTH), jnp.float32)
            for count in (share, 1, 1)
        ),
        in_specs=[plain] * len(sources),
        out_specs=(vmem,) * 3,
        scratch_shapes=[pltpu.VMEM((rows, width), jnp.bfloat16)] * len(layout)
        + [pltpu.SemaphoreType.DMA((len(layout),))],
        compiler_params=pltpu.CompilerParams(vmem_limit_bytes=65024 * 1024),
        cost_estimate=pl.CostEstimate(flops=1, bytes_accessed=1, transcendentals=0),
        name="total_terms",
    )(*sources)


def after(value, *others):
    return lax.optimization_barrier((value, *others))[0]


def up(value, first, last):
    return lax.ppermute(value, "dp", [(i, i + 1) for i in range(first, last)])


def down(value, first, last):
    return lax.ppermute(value, "dp", [(i + 1, i) for i in range(first, last)])


def add(*terms):
    return functools.reduce(lambda a, b: a + b, [term.astype(jnp.float32) for term in terms])


def link(value, *pairs):
    return lax.ppermute(value, "dp", pairs)


ENDS = ((0, 1), (3, 2))
OUTER = ((0, 1), (1, 0), (2, 3), (3, 2))
INNER = ((1, 2), (2, 1))
OUTWARD = ((1, 0), (2, 3))


def gather_four(parts):
    outer = [link(part, *OUTER) for part in parts]
    inner = [link(part, *INNER) for part in parts]
    inner_second = [link(part, *INNER) for part in outer]
    outer_second = [link(part, *OUTWARD) for part in inner]
    outer_third = [link(part, *OUTWARD) for part in inner_second]
    own = tuple((plane, plane) for plane in range(4))
    swap = tuple((plane, plane ^ 1) for plane in range(4))
    spots = (own, swap, ((1, 2), (2, 1)), ((1, 3), (2, 0)), ((0, 2), (3, 1)), ((0, 3), (3, 0)))
    columns = zip(parts, outer, inner, inner_second, outer_second, outer_third)
    return [piece for column in columns for piece in column], spots * len(parts)


def gather_line(block, planes):
    left, right = [block], [block]
    for step in range(planes - 1):
        left.append(up(left[-1], step, planes - 1))
        right.append(down(right[-1], 0, planes - 1 - step))
    spots = [tuple((plane, plane - hop) for plane in range(hop, planes)) for hop in range(planes)]
    spots += [
        tuple((plane, plane + hop) for plane in range(planes - hop)) for hop in range(1, planes)
    ]
    return left + right[1:], tuple(spots)


def stacked(terms, planes):
    return terms.reshape(planes, terms.shape[0] // planes, terms.shape[1])


def scatter_step(planes, step, terms, received, marks=()):
    ups, downs = scatter_cases(planes, step, 0, 1, 2)
    if step == 1:
        ups, downs = ups[:1], downs[:1]
    left, right = mix((ups, downs), (terms, *received), marks)
    received = up(left, 0, step), down(right, planes - 1 - step, planes - 1)
    return received, (left, right)


def exchange_cases(step, terms, outer, inner):
    place = 4 - step
    ends = [(0, 1, [(terms, place)]), (3, 4, [(terms, -place)])]
    if step == 1:
        return ends, []
    inward = [(1, 2, [(terms, place), (outer, None)]), (2, 3, [(terms, -place), (outer, None)])]
    outward = [(1, 2, [(terms, -place), (inner, None)]), (2, 3, [(terms, place), (inner, None)])]
    return ends + outward * (step == 3), inward


def exchange(step, terms, received, marks):
    outer, inner = mix(exchange_cases(step, 0, 1, 2), (terms, *received), marks)
    return (link(outer, *(OUTER if step == 3 else ENDS)), link(inner, *INNER)), (outer, inner)


def whole(planes, first):
    return [
        [(0, planes, first, True)],
        [(0, planes, first + 1, False)],
        [(0, planes, first + 2, False)],
    ]


def local(planes, owners, tokens, q_weight, key_projection, value_projection, q_gain, k_gain, doc_lengths, out_cot):
    groups = key_projection.shape[1] // HEAD_WIDTH
    share = q_weight.shape[1] // key_projection.shape[1]
    wide = share * HEAD_WIDTH
    row_tokens = lax.all_gather(tokens, "seq", axis=0, tiled=True)
    length, model = row_tokens.shape
    rows = length // owners
    tables = doc_tables(doc_lengths[0], length)
    gains = (q_gain[None, :], k_gain[None, :])
    me = lax.axis_index("seq")
    side, pair = lax.rem(me, 2), lax.div(me, 2)

    def halves(group):
        narrow = slice(group * HEAD_WIDTH, (group + 1) * HEAD_WIDTH)
        broad = slice(group * wide, (group + 1) * wide)
        return (
            q_weight[:, broad],
            jnp.concatenate([key_projection[:, narrow], value_projection[:, narrow]], axis=1),
        )

    def group_heads(group, pieces, spots, marks=(), parts=1):
        out, grad, weight, terms = heads(
            share, parts, pieces, spots, row_tokens, tables, gains, doc_lengths,
            out_cot[:, group * wide : (group + 1) * wide], marks,
        )
        return out, grad, weight, stacked(terms, planes)

    def token_part(which, grad, weight, adds=(), parts=(), marks=(), split=False):
        return token_terms(grad, weight, which, owners, adds, parts, marks, split)

    outs, layout, sources = [], [], []
    sent = kept = ()
    paired = groups == 2 and planes == 4
    if paired:
        pieces, spots = gather_four(halves(0))
        block = after(jnp.concatenate(halves(1), axis=1), pieces[4])
        far = link(block, (0, 2), (1, 3), (2, 0), (3, 1))
        block = after(block, pieces[5])
        near, middle = link(block, *OUTER), link(block, *INNER)
        out, grad, weight, terms = group_heads(0, pieces, spots, parts=2)
        outs.append(out)
        (first,) = mix((exchange_cases(1, 0, None, None)[0],), (terms,), ())
        received = (link(first, *ENDS),)
        sent = (token_part(1 - side, grad, weight, marks=(first, far)),)
        last = link(far, *OUTWARD)
        outer_cases, inner_cases = exchange_cases(2, 0, 1, None)
        edges = [(0, 1, [(0, 1)]), (3, 4, [(0, -1)])]
        outer, inner, edge = mix((outer_cases, inner_cases, edges), (terms, *received), (*sent, near, middle))
        received = link(outer, *ENDS), link(inner, *INNER)
        edge_received = link(edge, *ENDS)
        old, early, marks = terms, (grad, weight), (outer, inner, edge)
        pieces = [block, near, middle, far, last]
        spots = (
            tuple((plane, plane) for plane in range(4)),
            tuple((plane, plane ^ 1) for plane in range(4)),
            ((1, 2), (2, 1)),
            tuple((plane, plane ^ 2) for plane in range(4)),
            ((0, 3), (3, 0)),
        )
        out, grad, weight, terms = group_heads(1, pieces, spots, marks)
        outs.append(out)
        outer_cases, inner_cases = exchange_cases(3, 0, 1, 2)
        outer_cases = exchange_cases(1, 3, None, None)[0] + outer_cases[2:]
        marks = mix((outer_cases, inner_cases), (old, *received, terms), ())
        received = link(marks[0], *OUTER), link(marks[1], *INNER)
        layout = [
            [(0, 4, 0, True)],
            [(0, 4, 1, False)],
            [(0, 1, 2, False), (1, 3, 3, False), (3, 4, 2, False)],
        ]
        sources = [old, edge_received, *received]
    else:
        for group in range(groups):
            block = jnp.concatenate(halves(group), axis=1)
            out, grad, weight, terms = group_heads(group, *gather_line(block, planes))
            outs.append(out)
            received, marks = scatter_step(planes, 1, terms, ())
            if group + 1 < groups:
                for step in range(2, planes):
                    received, marks = scatter_step(planes, step, terms, received)
                layout += whole(planes, len(sources))
                sources += [terms, *received]
                sent = (token_part(1 - side, grad, weight, sent),)
                kept = (token_part(side, grad, weight, kept),)
    sent = token_part(1 - side, grad, weight, sent, marks=marks, split=True)
    swapped = [lax.ppermute(part, "seq", [(i, i ^ 1) for i in range(owners)]) for part in sent]
    forward = functools.partial(scatter_step, planes)
    if paired:
        kept = (token_part(side, *early, marks=sent),)
        forward = exchange
    received, marks = forward(2, terms, received[:1] if paired else received, kept)
    kept = token_part(side, grad, weight, kept, swapped, marks)
    shares = [lax.dynamic_index_in_dim(kept, pair, 0, keepdims=False)]
    for other in range(1, owners // 2):
        part = lax.dynamic_index_in_dim(kept, pair ^ other, 0, keepdims=False)
        shares.append(lax.ppermute(part, "seq", [(i, i ^ (2 * other)) for i in range(owners)]))
    marks = (kept,)
    for step in range(3, planes):
        received, marks = forward(step, terms, received, marks)
    spread = lax.all_to_all(
        after(jnp.concatenate(outs, axis=1), *marks),
        "seq",
        split_axis=0,
        concat_axis=0,
        tiled=True,
    )
    layout += whole(planes, len(sources))
    sources += [terms, *received]
    weight_grads = total_terms(share, layout, sources)
    token_grad = add(*shares).astype(jnp.bfloat16)
    attn_out = spread.reshape(owners, rows, groups * wide).transpose(1, 0, 2)
    attn_out = attn_out.reshape(rows, owners * groups * wide)
    return (attn_out, token_grad, *weight_grads)


def solution(mesh):
    rows, split = P(("dp", "seq"), None), P("dp", "seq")
    return jax.shard_map(
        functools.partial(local, mesh.shape["dp"], mesh.shape["seq"]),
        mesh=mesh,
        in_specs=(rows, split, split, split, P(), P(), P("dp", None), split),
        out_specs=(rows, rows, split, split, split),
        check_vma=False,
    )
```

profile of v0, /device:TPU:0, one launch (start us, length us, event | category | flops | bytes accessed | tf_op | source)
XLA Modules:
  0.0 239.0 jit_solution(13282507568296562745)
XLA Ops:
  9.2 3.1 %collective-permute-start.5 = (bf16[672,256]{1,0:T(8,128)(2,1)S(1)}, bf16[672,256]{1,0:T(8,128)(2,1)S(1)}, u32[]{:S(2)}, u32[]{:S(2)}) collective-permute-start(bf16[672,256]{1,0:T(8,128)(2,1)S(1)} %pad_maximum_fusion.4.refs_6_), channel_id=1, source_target_pairs={{0,8},{8,0},{16,24},{24,16},{1,9},{9,1},{17,25},{25,17},{2,10},{10... | collective-permute-start | bytes 1032200 | tf_op jit(solution)/shard_map/ppermute | solution.py:423
  13.0 4.4 %collective-permute-start = (bf16[672,256]{1,0:T(8,128)(2,1)S(1)}, bf16[672,256]{1,0:T(8,128)(2,1)S(1)}, u32[]{:S(2)}, u32[]{:S(2)}) collective-permute-start(bf16[672,256]{1,0:T(8,128)(2,1)S(1)} %get-tuple-element.64.refs_0_), channel_id=1, source_target_pairs={{0,8},{8,0},{16,24},{24,16},{1,9},{9,1},{17,25},{25,17},{2,10},{10... | collective-permute-start | bytes 1032200 | tf_op jit(solution)/shard_map/ppermute | solution.py:423
  18.5 2.7 %collective-permute-done.5.refs_7_ = bf16[672,256]{1,0:T(8,128)(2,1)S(1)} collective-permute-done((bf16[672,256]{1,0:T(8,128)(2,1)S(1)}, bf16[672,256]{1,0:T(8,128)(2,1)S(1)}, u32[]{:S(2)}, u32[]{:S(2)}) %collective-permute-start.5) | collective-permute-done | bytes 344096 | tf_op jit(solution)/shard_map/ppermute | solution.py:423
  21.9 5.9 %collective-permute-done.refs_1_ = bf16[672,256]{1,0:T(8,128)(2,1)S(1)} collective-permute-done((bf16[672,256]{1,0:T(8,128)(2,1)S(1)}, bf16[672,256]{1,0:T(8,128)(2,1)S(1)}, u32[]{:S(2)}, u32[]{:S(2)}) %collective-permute-start) | collective-permute-done | bytes 344096 | tf_op jit(solution)/shard_map/ppermute | solution.py:423
  28.4 1.9 fusion.3
  38.9 14.9 %collective-permute-done.3.refs_4_ = bf16[672,256]{1,0:T(8,128)(2,1)S(1)} collective-permute-done((bf16[672,256]{1,0:T(8,128)(2,1)S(1)}, bf16[672,256]{1,0:T(8,128)(2,1)S(1)}, u32[]{:S(2)}, u32[]{:S(2)}) %collective-permute-start.3) | collective-permute-done | bytes 344096 | tf_op jit(solution)/shard_map/ppermute | solution.py:423
  53.9 12.9 %collective-permute-done.4.refs_5_ = bf16[672,256]{1,0:T(8,128)(2,1)S(1)} collective-permute-done((bf16[672,256]{1,0:T(8,128)(2,1)S(1)}, bf16[672,256]{1,0:T(8,128)(2,1)S(1)}, u32[]{:S(2)}, u32[]{:S(2)}) %collective-permute-start.4) | collective-permute-done | bytes 344096 | tf_op jit(solution)/shard_map/ppermute | solution.py:423
  66.7 1.5 collective-permute-start.11
  69.1 24.2 %heads.2 = (bf16[1024,256]{1,0:T(8,128)(2,1)}, bf16[1024,512]{1,0:T(8,128)(2,1)}, bf16[2688,512]{1,0:T(8,128)(2,1)}, bf16[2688,512]{1,0:T(8,128)(2,1)}) custom-call(s32[1,4]{1,0:T(1,128)} %lengths_ref.3, f32[1,128]{1,0:T(1,128)} %bitcast.45, f32[1,128]{1,0:T(1,128)} %bitcast.47, bf16[672,256]{1,0:T(8,128)(2,1)} %copy-done.6, bf16[672,256]{1,0:T(8,128)(2,1)} %copy-done.11, ...), custom_call_target="tpu_custom_call" | custom-call | flops 8858370048 | bytes 17956864 | tf_op jit(solution)/shard_map/heads/pallas_call | solution.py:200
  93.3 2.0 mix.5.refs_0_
  95.3 5.7 %collective-permute-start.14 = (bf16[672,512]{1,0:T(8,128)(2,1)}, bf16[672,512]{1,0:T(8,128)(2,1)}, u32[]{:S(2)}, u32[]{:S(2)}) collective-permute-start(bf16[672,512]{1,0:T(8,128)(2,1)} %mix.5.refs_0_), channel_id=1, source_target_pairs={{0,8},{24,16},{1,9},{25,17},{2,10},{26,18},{3,11},{27,19},{4,12},{... | collective-permute-start | bytes 2064392 | tf_op jit(solution)/shard_map/ppermute | solution.py:423
  102.3 4.9 %token_terms.4.refs_2_.refs_0_ = bf16[4,128,2688]{2,1,0:T(8,128)(2,1)} custom-call(s32[1]{0:T(128)} %bitcast.7.side_ref, bf16[4,2,128,512]{3,2,1,0:T(8,128)(2,1)} %bitcast.37, bf16[2688,512]{1,0:T(8,128)(2,1)} %get-tuple-element.37.weight_ref, bf16[672,512]{1,0:T(8,128)(2,1)} %mix.5.refs_0_, bf16[672,512]{1,0:T(8,128)(2,1)} %collective-permute-done.12.refs_1_.refs_3_), custom_call_target="tpu_custom_call" | custom-call | flops 524288 | bytes 524288 | tf_op jit(solution)/shard_map/token_terms/pallas_call | solution.py:275
  107.2 5.6 %collective-permute-done.14.refs_1_ = bf16[672,512]{1,0:T(8,128)(2,1)} collective-permute-done((bf16[672,512]{1,0:T(8,128)(2,1)}, bf16[672,512]{1,0:T(8,128)(2,1)}, u32[]{:S(2)}, u32[]{:S(2)}) %collective-permute-start.14) | collective-permute-done | bytes 688160 | tf_op jit(solution)/shard_map/ppermute | solution.py:423
  112.8 2.7 %mix.6 = (bf16[672,512]{1,0:T(8,128)(2,1)}, bf16[672,512]{1,0:T(8,128)(2,1)}, bf16[672,512]{1,0:T(8,128)(2,1)}) custom-call(bf16[4,672,512]{2,1,0:T(8,128)(2,1)} %bitcast.34, bf16[672,512]{1,0:T(8,128)(2,1)} %collective-permute-done.14.refs_1_, bf16[4,128,2688]{2,1,0:T(8,128)(2,1)} %token_terms.4.refs_2_.refs_0_, ...), custom_call_target="tpu_custom_call" | custom-call | flops 1 | bytes 1 | tf_op jit(solution)/shard_map/mix/pallas_call | solution.py:338
  115.5 5.4 %collective-permute-start.15 = (bf16[672,512]{1,0:T(8,128)(2,1)}, bf16[672,512]{1,0:T(8,128)(2,1)}, u32[]{:S(2)}, u32[]{:S(2)}) collective-permute-start(bf16[672,512]{1,0:T(8,128)(2,1)} %get-tuple-element.38.refs_9_), channel_id=1, source_target_pairs={{0,8},{24,16},{1,9},{25,17},{2,10},{26,18},{3,11},{27,19},{4,12},{... | collective-permute-start | bytes 2064392 | tf_op jit(solution)/shard_map/ppermute | solution.py:423
  122.4 24.1 %heads.3 = (bf16[1024,256]{1,0:T(8,128)(2,1)}, bf16[1024,512]{1,0:T(8,128)(2,1)}, bf16[2688,512]{1,0:T(8,128)(2,1)}, bf16[2688,512]{1,0:T(8,128)(2,1)}) custom-call(s32[1,4]{1,0:T(1,128)} %lengths_ref.3, f32[1,128]{1,0:T(1,128)} %bitcast.46, f32[1,128]{1,0:T(1,128)} %bitcast.48, bf16[672,512]{1,0:T(8,128)(2,1)} %pad_maximum_fusion.1.refs_0_, ...), custom_call_target="tpu_custom_call" | custom-call | flops 8858370048 | bytes 17956864 | tf_op jit(solution)/shard_map/heads/pallas_call | solution.py:200
  146.5 2.2 mix.7
  149.9 6.0 %token_terms.5 = (bf16[128,2688]{1,0:T(8,128)(2,1)}, bf16[128,2688]{1,0:T(8,128)(2,1)}, bf16[128,2688]{1,0:T(8,128)(2,1)}, bf16[128,2688]{1,0:T(8,128)(2,1)}) custom-call(s32[1]{0:T(128)} %bitcast.7.side_ref, bf16[4,2,128,512]{3,2,1,0:T(8,128)(2,1)} %bitcast.40, bf16[2688,512]{1,0:T(8,128)(2,1)} %get-tuple-element.45.weight_ref, ...), custom_call_target="tpu_custom_call" | custom-call | flops 524288 | bytes 524288 | tf_op jit(solution)/shard_map/token_terms/pallas_call | solution.py:275
  157.0 4.9 %token_terms.6.refs_2_.refs_0_ = bf16[4,128,2688]{2,1,0:T(8,128)(2,1)} custom-call(s32[1]{0:T(128)} %bitcast.10.side_ref, bf16[4,2,128,512]{3,2,1,0:T(8,128)(2,1)} %bitcast.38, bf16[2688,512]{1,0:T(8,128)(2,1)} %get-tuple-element.37.weight_ref, bf16[128,2688]{1,0:T(8,128)(2,1)} %get-tuple-element.47.refs_0_, bf16[128,2688]{1,0:T(8,128)(2,1)} %get-tuple-element.48.refs_1_, ...), custom_call_target="tpu_custom_call" | custom-call | flops 524288 | bytes 524288 | tf_op jit(solution)/shard_map/token_terms/pallas_call | solution.py:275
  162.8 2.2 mix.8
  165.1 4.5 %collective-permute-start.18 = (bf16[672,512]{1,0:T(8,128)(2,1)}, bf16[672,512]{1,0:T(8,128)(2,1)}, u32[]{:S(2)}, u32[]{:S(2)}) collective-permute-start(bf16[672,512]{1,0:T(8,128)(2,1)} %get-tuple-element.51.refs_5_), channel_id=1, source_target_pairs={{0,8},{24,16},{1,9},{25,17},{2,10},{26,18},{3,11},{27,19},{4,12},{... | collective-permute-start | bytes 2064392 | tf_op jit(solution)/shard_map/ppermute | solution.py:423
  169.6 1.5 collective-permute-start.19
  171.1 6.6 %token_terms.7.refs_3_ = bf16[4,128,2688]{2,1,0:T(8,128)(2,1)} custom-call(s32[1]{0:T(128)} %bitcast.10.side_ref, bf16[4,2,128,512]{3,2,1,0:T(8,128)(2,1)} %bitcast.41, bf16[2688,512]{1,0:T(8,128)(2,1)} %get-tuple-element.45.weight_ref, bf16[4,128,2688]{2,1,0:T(8,128)(2,1)} %token_terms.6.refs_2_.refs_0_, bf16[128,2688]{1,0:T(8,128)(2,1)} %collective-permute-done.20.refs_1_, ...), custom_call_target="tpu_custom_call" | custom-call | flops 524288 | bytes 524288 | tf_op jit(solution)/shard_map/token_terms/pallas_call | solution.py:275
  177.7 3.0 %dynamic-slice_bitcast_fusion.2 = (bf16[128,2688]{1,0:T(8,128)(2,1)}, bf16[128,2688]{1,0:T(8,128)(2,1)}, bf16[128,2688]{1,0:T(8,128)(2,1)}) fusion(bf16[4,128,2688]{2,1,0:T(8,128)(2,1)} %token_terms.7.refs_3_, s32[]{:T(128)S(6)} %select_n.19, s32[]{:T(128)S(6)} %select_n.21, s32[]{:T(128)S(6)} %select_n.20), kind=kLoop, calls=%fused_computation.10 | loop fusion | bytes 4128780 | tf_op jit(solution)/shard_map/jit(dynamic_index_in_dim)/squeeze | solution.py:587
  185.2 2.2 mix.9
  187.5 4.4 %all-to-all-start = ((bf16[8,128,512]{2,1,0:T(8,128)(2,1)}), bf16[8,128,512]{2,1,0:T(8,128)(2,1)}, u32[]{:S(2)}, u32[]{:S(2)}) async-start(bf16[8,128,512]{2,1,0:T(8,128)(2,1)} %bitcast.39), calls=%async_computation | async-start | bytes 2097152 | tf_op jit(solution)/shard_map/all_to_all | solution.py:592
  191.9 4.8 %collective-permute-start.27 = (bf16[672,512]{1,0:T(8,128)(2,1)S(1)}, bf16[672,512]{1,0:T(8,128)(2,1)}, u32[]{:S(2)}, u32[]{:S(2)}) collective-permute-start(bf16[672,512]{1,0:T(8,128)(2,1)S(1)} %copy-done.7), channel_id=1, source_target_pairs={{0,8},{24,16},{1,9},{25,17},{2,10},{26,18},{3,11},{27,19},{4,12},{... | collective-permute-start | bytes 2064392 | tf_op jit(solution)/shard_map/ppermute | solution.py:423
  199.4 17.6 %collective-permute-done.25 = bf16[128,2688]{1,0:T(8,128)(2,1)} collective-permute-done((bf16[128,2688]{1,0:T(8,128)(2,1)}, bf16[128,2688]{1,0:T(8,128)(2,1)}, u32[]{:S(2)}, u32[]{:S(2)}) %collective-permute-start.25) | collective-permute-done | bytes 688160 | tf_op jit(solution)/shard_map/ppermute | solution.py:588
  218.5 2.9 %fusion.2 = bf16[128,2688]{1,0:T(8,128)(2,1)} fusion(bf16[128,2688]{1,0:T(8,128)(2,1)} %collective-permute-done.26, bf16[128,2688]{1,0:T(8,128)(2,1)} %collective-permute-done.25, bf16[128,2688]{1,0:T(8,128)(2,1)} %collective-permute-done.24, bf16[4,128,2688]{2,1,0:T(8,128)(2,1)} %token_terms.7.refs_3_, s32[]{:T(128)S(6)} %select_n.18), kind=kLoop, calls=%fused_computation.3 | loop fusion | flops 2752512 | bytes 3440644 | tf_op jit(solution)/shard_map/convert_element_type | solution.py:602
  221.5 4.5 %collective-permute-done.29.refs_5_ = bf16[672,512]{1,0:T(8,128)(2,1)} collective-permute-done((bf16[672,512]{1,0:T(8,128)(2,1)}, bf16[672,512]{1,0:T(8,128)(2,1)}, u32[]{:S(2)}, u32[]{:S(2)}) %collective-permute-start.29) | collective-permute-done | bytes 688160 | tf_op jit(solution)/shard_map/ppermute | solution.py:423
  226.0 3.9 %total_terms.1 = (f32[672,512]{1,0:T(8,128)}, f32[672,256]{1,0:T(8,128)}, f32[672,256]{1,0:T(8,128)}) custom-call(bf16[4,672,512]{2,1,0:T(8,128)(2,1)} %bitcast.36, bf16[672,512]{1,0:T(8,128)(2,1)} %collective-permute-done.27.refs_1_, bf16[672,512]{1,0:T(8,128)(2,1)} %collective-permute-done.17.refs_1_.refs_2_, ...), custom_call_target="tpu_custom_call" | custom-call | flops 1 | bytes 1 | tf_op jit(solution)/shard_map/total_terms/pallas_call | solution.py:390
  229.9 2.3 copy.15
  (103 shorter events, 29.0 us)
Async XLA Ops:
  7.2 61.2 %all-gather.2.cloned.1.call-start = ((), (), s32[]{:S(2)}) async-start(), calls=%async_computation.1 | async-start | bytes 6193152 | tf_op jit(solution)/shard_map/all_gather | solution.py:497
  9.2 12.0 %collective-permute-start.5 = (bf16[672,256]{1,0:T(8,128)(2,1)S(1)}, bf16[672,256]{1,0:T(8,128)(2,1)S(1)}, u32[]{:S(2)}, u32[]{:S(2)}) collective-permute-start(bf16[672,256]{1,0:T(8,128)(2,1)S(1)} %pad_maximum_fusion.4.refs_6_), channel_id=1, source_target_pairs={{0,8},{8,0},{16,24},{24,16},{1,9},{9,1},{17,25},{25,17},{2,10},{10... | collective-permute-start | bytes 1032200 | tf_op jit(solution)/shard_map/ppermute | solution.py:423
  12.3 19.4 %collective-permute-start.6 = (bf16[672,256]{1,0:T(8,128)(2,1)S(1)}, bf16[672,256]{1,0:T(8,128)(2,1)S(1)}, u32[]{:S(2)}, u32[]{:S(2)}) collective-permute-start(bf16[672,256]{1,0:T(8,128)(2,1)S(1)} %pad_maximum_fusion.4.refs_6_), channel_id=1, source_target_pairs={{8,16},{16,8},{9,17},{17,9},{10,18},{18,10},{11,19},{19,11},{12,20... | collective-permute-start | bytes 1032200 | tf_op jit(solution)/shard_map/ppermute | solution.py:423
  13.0 14.7 %collective-permute-start = (bf16[672,256]{1,0:T(8,128)(2,1)S(1)}, bf16[672,256]{1,0:T(8,128)(2,1)S(1)}, u32[]{:S(2)}, u32[]{:S(2)}) collective-permute-start(bf16[672,256]{1,0:T(8,128)(2,1)S(1)} %get-tuple-element.64.refs_0_), channel_id=1, source_target_pairs={{0,8},{8,0},{16,24},{24,16},{1,9},{9,1},{17,25},{25,17},{2,10},{10... | collective-permute-start | bytes 1032200 | tf_op jit(solution)/shard_map/ppermute | solution.py:423
  17.5 15.5 %collective-permute-start.1 = (bf16[672,256]{1,0:T(8,128)(2,1)S(1)}, bf16[672,256]{1,0:T(8,128)(2,1)S(1)}, u32[]{:S(2)}, u32[]{:S(2)}) collective-permute-start(bf16[672,256]{1,0:T(8,128)(2,1)S(1)} %get-tuple-element.64.refs_0_), channel_id=1, source_target_pairs={{8,16},{16,8},{9,17},{17,9},{10,18},{18,10},{11,19},{19,11},{12,20... | collective-permute-start | bytes 1032200 | tf_op jit(solution)/shard_map/ppermute | solution.py:423
  21.2 13.1 %collective-permute-start.7 = (bf16[672,256]{1,0:T(8,128)(2,1)S(1)}, bf16[672,256]{1,0:T(8,128)(2,1)S(1)}, u32[]{:S(2)}, u32[]{:S(2)}) collective-permute-start(bf16[672,256]{1,0:T(8,128)(2,1)S(1)} %collective-permute-done.5.refs_7_), channel_id=1, source_target_pairs={{8,16},{16,8},{9,17},{17,9},{10,18},{18,10},{11,19},{19,11},{12,20... | collective-permute-start | bytes 1032200 | tf_op jit(solution)/shard_map/ppermute | solution.py:423
  31.7 36.6 %collective-permute-start.8 = (bf16[672,256]{1,0:T(8,128)(2,1)S(1)}, bf16[672,256]{1,0:T(8,128)(2,1)S(1)}, u32[]{:S(2)}, u32[]{:S(2)}) collective-permute-start(bf16[672,256]{1,0:T(8,128)(2,1)S(1)} %collective-permute-done.6.refs_8_), channel_id=1, source_target_pairs={{8,0},{16,24},{9,1},{17,25},{10,2},{18,26},{11,3},{19,27},{12,4},{... | collective-permute-start | bytes 1032200 | tf_op jit(solution)/shard_map/ppermute | solution.py:423
  33.0 20.8 %collective-permute-start.3 = (bf16[672,256]{1,0:T(8,128)(2,1)S(1)}, bf16[672,256]{1,0:T(8,128)(2,1)S(1)}, u32[]{:S(2)}, u32[]{:S(2)}) collective-permute-start(bf16[672,256]{1,0:T(8,128)(2,1)S(1)} %collective-permute-done.1.refs_2_), channel_id=1, source_target_pairs={{8,0},{16,24},{9,1},{17,25},{10,2},{18,26},{11,3},{19,27},{12,4},{... | collective-permute-start | bytes 1032200 | tf_op jit(solution)/shard_map/ppermute | solution.py:423
  34.3 34.0 %collective-permute-start.9 = (bf16[672,256]{1,0:T(8,128)(2,1)S(1)}, bf16[672,256]{1,0:T(8,128)(2,1)S(1)}, u32[]{:S(2)}, u32[]{:S(2)}) collective-permute-start(bf16[672,256]{1,0:T(8,128)(2,1)S(1)} %collective-permute-done.7.refs_9_), channel_id=1, source_target_pairs={{8,0},{16,24},{9,1},{17,25},{10,2},{18,26},{11,3},{19,27},{12,4},{... | collective-permute-start | bytes 1032200 | tf_op jit(solution)/shard_map/ppermute | solution.py:423
  35.6 31.1 %collective-permute-start.4 = (bf16[672,256]{1,0:T(8,128)(2,1)S(1)}, bf16[672,256]{1,0:T(8,128)(2,1)S(1)}, u32[]{:S(2)}, u32[]{:S(2)}) collective-permute-start(bf16[672,256]{1,0:T(8,128)(2,1)S(1)} %collective-permute-done.2.refs_3_), channel_id=1, source_target_pairs={{8,0},{16,24},{9,1},{17,25},{10,2},{18,26},{11,3},{19,27},{12,4},{... | collective-permute-start | bytes 1032200 | tf_op jit(solution)/shard_map/ppermute | solution.py:423
  53.9 47.1 %collective-permute-start.12 = (bf16[672,512]{1,0:T(8,128)(2,1)}, bf16[672,512]{1,0:T(8,128)(2,1)}, u32[]{:S(2)}, u32[]{:S(2)}) collective-permute-start(bf16[672,512]{1,0:T(8,128)(2,1)} %pad_maximum_fusion.1.refs_0_), channel_id=1, source_target_pairs={{0,16},{8,24},{16,0},{24,8},{1,17},{9,25},{17,1},{25,9},{2,18},{10... | collective-permute-start | bytes 2064392 | tf_op jit(solution)/shard_map/ppermute | solution.py:423
  66.7 40.5 %collective-permute-start.10 = (bf16[672,512]{1,0:T(8,128)(2,1)}, bf16[672,512]{1,0:T(8,128)(2,1)}, u32[]{:S(2)}, u32[]{:S(2)}) collective-permute-start(bf16[672,512]{1,0:T(8,128)(2,1)} %pad_maximum_fusion.1.refs_0_), channel_id=1, source_target_pairs={{0,8},{8,0},{16,24},{24,16},{1,9},{9,1},{17,25},{25,17},{2,10},{10... | collective-permute-start | bytes 2064392 | tf_op jit(solution)/shard_map/ppermute | solution.py:423
  66.7 40.5 %collective-permute-start.11 = (bf16[672,512]{1,0:T(8,128)(2,1)}, bf16[672,512]{1,0:T(8,128)(2,1)}, u32[]{:S(2)}, u32[]{:S(2)}) collective-permute-start(bf16[672,512]{1,0:T(8,128)(2,1)} %pad_maximum_fusion.1.refs_0_), channel_id=1, source_target_pairs={{8,16},{16,8},{9,17},{17,9},{10,18},{18,10},{11,19},{19,11},{12,20... | collective-permute-start | bytes 2064392 | tf_op jit(solution)/shard_map/ppermute | solution.py:423
  95.3 17.5 %collective-permute-start.14 = (bf16[672,512]{1,0:T(8,128)(2,1)}, bf16[672,512]{1,0:T(8,128)(2,1)}, u32[]{:S(2)}, u32[]{:S(2)}) collective-permute-start(bf16[672,512]{1,0:T(8,128)(2,1)} %mix.5.refs_0_), channel_id=1, source_target_pairs={{0,8},{24,16},{1,9},{25,17},{2,10},{26,18},{3,11},{27,19},{4,12},{... | collective-permute-start | bytes 2064392 | tf_op jit(solution)/shard_map/ppermute | solution.py:423
  101.0 21.5 %collective-permute-start.13 = (bf16[672,512]{1,0:T(8,128)(2,1)}, bf16[672,512]{1,0:T(8,128)(2,1)}, u32[]{:S(2)}, u32[]{:S(2)}) collective-permute-start(bf16[672,512]{1,0:T(8,128)(2,1)} %collective-permute-done.12.refs_1_.refs_3_), channel_id=1, source_target_pairs={{8,0},{16,24},{9,1},{17,25},{10,2},{18,26},{11,3},{19,27},{12,4},{... | collective-permute-start | bytes 2064392 | tf_op jit(solution)/shard_map/ppermute | solution.py:423
  115.5 31.0 %collective-permute-start.15 = (bf16[672,512]{1,0:T(8,128)(2,1)}, bf16[672,512]{1,0:T(8,128)(2,1)}, u32[]{:S(2)}, u32[]{:S(2)}) collective-permute-start(bf16[672,512]{1,0:T(8,128)(2,1)} %get-tuple-element.38.refs_9_), channel_id=1, source_target_pairs={{0,8},{24,16},{1,9},{25,17},{2,10},{26,18},{3,11},{27,19},{4,12},{... | collective-permute-start | bytes 2064392 | tf_op jit(solution)/shard_map/ppermute | solution.py:423
  120.9 25.6 %collective-permute-start.16 = (bf16[672,512]{1,0:T(8,128)(2,1)}, bf16[672,512]{1,0:T(8,128)(2,1)}, u32[]{:S(2)}, u32[]{:S(2)}) collective-permute-start(bf16[672,512]{1,0:T(8,128)(2,1)} %get-tuple-element.39.refs_10_), channel_id=1, source_target_pairs={{8,16},{16,8},{9,17},{17,9},{10,18},{18,10},{11,19},{19,11},{12,20... | collective-permute-start | bytes 2064392 | tf_op jit(solution)/shard_map/ppermute | solution.py:423
  148.8 14.1 %collective-permute-start.17 = (bf16[672,512]{1,0:T(8,128)(2,1)}, bf16[672,512]{1,0:T(8,128)(2,1)}, u32[]{:S(2)}, u32[]{:S(2)}) collective-permute-start(bf16[672,512]{1,0:T(8,128)(2,1)} %get-tuple-element.43.refs_1_), channel_id=1, source_target_pairs={{0,8},{8,0},{16,24},{24,16},{1,9},{9,1},{17,25},{25,17},{2,10},{10... | collective-permute-start | bytes 2064392 | tf_op jit(solution)/shard_map/ppermute | solution.py:423
  156.0 13.6 %collective-permute-start.20 = (bf16[128,2688]{1,0:T(8,128)(2,1)}, bf16[128,2688]{1,0:T(8,128)(2,1)}, u32[]{:S(2)}, u32[]{:S(2)}) collective-permute-start(bf16[128,2688]{1,0:T(8,128)(2,1)} %get-tuple-element.47.refs_0_), channel_id=1, source_target_pairs={{0,1},{1,0},{2,3},{3,2},{4,5},{5,4},{6,7},{7,6},{8,9},{9,8},{10,11... | collective-permute-start | bytes 2064392 | tf_op jit(solution)/shard_map/ppermute | solution.py:578
  156.0 15.2 %collective-permute-start.21 = (bf16[128,2688]{1,0:T(8,128)(2,1)}, bf16[128,2688]{1,0:T(8,128)(2,1)}, u32[]{:S(2)}, u32[]{:S(2)}) collective-permute-start(bf16[128,2688]{1,0:T(8,128)(2,1)} %get-tuple-element.48.refs_1_), channel_id=1, source_target_pairs={{0,1},{1,0},{2,3},{3,2},{4,5},{5,4},{6,7},{7,6},{8,9},{9,8},{10,11... | collective-permute-start | bytes 2064392 | tf_op jit(solution)/shard_map/ppermute | solution.py:578
  156.5 14.7 %collective-permute-start.22 = (bf16[128,2688]{1,0:T(8,128)(2,1)}, bf16[128,2688]{1,0:T(8,128)(2,1)}, u32[]{:S(2)}, u32[]{:S(2)}) collective-permute-start(bf16[128,2688]{1,0:T(8,128)(2,1)} %get-tuple-element.49.refs_2_), channel_id=1, source_target_pairs={{0,1},{1,0},{2,3},{3,2},{4,5},{5,4},{6,7},{7,6},{8,9},{9,8},{10,11... | collective-permute-start | bytes 2064392 | tf_op jit(solution)/shard_map/ppermute | solution.py:578
  156.5 14.7 %collective-permute-start.23 = (bf16[128,2688]{1,0:T(8,128)(2,1)}, bf16[128,2688]{1,0:T(8,128)(2,1)}, u32[]{:S(2)}, u32[]{:S(2)}) collective-permute-start(bf16[128,2688]{1,0:T(8,128)(2,1)} %get-tuple-element.50.refs_3_), channel_id=1, source_target_pairs={{0,1},{1,0},{2,3},{3,2},{4,5},{5,4},{6,7},{7,6},{8,9},{9,8},{10,11... | collective-permute-start | bytes 2064392 | tf_op jit(solution)/shard_map/ppermute | solution.py:578
  165.1 20.2 %collective-permute-start.18 = (bf16[672,512]{1,0:T(8,128)(2,1)}, bf16[672,512]{1,0:T(8,128)(2,1)}, u32[]{:S(2)}, u32[]{:S(2)}) collective-permute-start(bf16[672,512]{1,0:T(8,128)(2,1)} %get-tuple-element.51.refs_5_), channel_id=1, source_target_pairs={{0,8},{24,16},{1,9},{25,17},{2,10},{26,18},{3,11},{27,19},{4,12},{... | collective-permute-start | bytes 2064392 | tf_op jit(solution)/shard_map/ppermute | solution.py:423
  169.6 15.6 %collective-permute-start.19 = (bf16[672,512]{1,0:T(8,128)(2,1)}, bf16[672,512]{1,0:T(8,128)(2,1)}, u32[]{:S(2)}, u32[]{:S(2)}) collective-permute-start(bf16[672,512]{1,0:T(8,128)(2,1)} %get-tuple-element.52.refs_6_), channel_id=1, source_target_pairs={{8,16},{16,8},{9,17},{17,9},{10,18},{18,10},{11,19},{19,11},{12,20... | collective-permute-start | bytes 2064392 | tf_op jit(solution)/shard_map/ppermute | solution.py:423
  180.7 18.7 %collective-permute-start.24 = (bf16[128,2688]{1,0:T(8,128)(2,1)}, bf16[128,2688]{1,0:T(8,128)(2,1)}, u32[]{:S(2)}, u32[]{:S(2)}) collective-permute-start(bf16[128,2688]{1,0:T(8,128)(2,1)} %get-tuple-element.59), channel_id=1, source_target_pairs={{0,2},{1,3},{2,0},{3,1},{4,6},{5,7},{6,4},{7,5},{8,10},{9,11},{10,... | collective-permute-start | bytes 2064392 | tf_op jit(solution)/shard_map/ppermute | solution.py:588
  182.2 34.8 %collective-permute-start.25 = (bf16[128,2688]{1,0:T(8,128)(2,1)}, bf16[128,2688]{1,0:T(8,128)(2,1)}, u32[]{:S(2)}, u32[]{:S(2)}) collective-permute-start(bf16[128,2688]{1,0:T(8,128)(2,1)} %get-tuple-element.61), channel_id=1, source_target_pairs={{0,4},{1,5},{2,6},{3,7},{4,0},{5,1},{6,2},{7,3},{8,12},{9,13},{10,... | collective-permute-start | bytes 2064392 | tf_op jit(solution)/shard_map/ppermute | solution.py:588
  183.7 34.8 %collective-permute-start.26 = (bf16[128,2688]{1,0:T(8,128)(2,1)}, bf16[128,2688]{1,0:T(8,128)(2,1)}, u32[]{:S(2)}, u32[]{:S(2)}) collective-permute-start(bf16[128,2688]{1,0:T(8,128)(2,1)} %get-tuple-element.60), channel_id=1, source_target_pairs={{0,6},{1,7},{2,4},{3,5},{4,2},{5,3},{6,0},{7,1},{8,14},{9,15},{10,... | collective-permute-start | bytes 2064392 | tf_op jit(solution)/shard_map/ppermute | solution.py:588
  187.5 42.4 %all-to-all-start = ((bf16[8,128,512]{2,1,0:T(8,128)(2,1)}), bf16[8,128,512]{2,1,0:T(8,128)(2,1)}, u32[]{:S(2)}, u32[]{:S(2)}) async-start(bf16[8,128,512]{2,1,0:T(8,128)(2,1)} %bitcast.39), calls=%async_computation | async-start | bytes 2097152 | tf_op jit(solution)/shard_map/all_to_all | solution.py:592
  191.9 29.5 %collective-permute-start.27 = (bf16[672,512]{1,0:T(8,128)(2,1)S(1)}, bf16[672,512]{1,0:T(8,128)(2,1)}, u32[]{:S(2)}, u32[]{:S(2)}) collective-permute-start(bf16[672,512]{1,0:T(8,128)(2,1)S(1)} %copy-done.7), channel_id=1, source_target_pairs={{0,8},{24,16},{1,9},{25,17},{2,10},{26,18},{3,11},{27,19},{4,12},{... | collective-permute-start | bytes 2064392 | tf_op jit(solution)/shard_map/ppermute | solution.py:423
  196.8 24.7 %collective-permute-start.28 = (bf16[672,512]{1,0:T(8,128)(2,1)S(1)}, bf16[672,512]{1,0:T(8,128)(2,1)}, u32[]{:S(2)}, u32[]{:S(2)}) collective-permute-start(bf16[672,512]{1,0:T(8,128)(2,1)S(1)} %copy-done.2), channel_id=1, source_target_pairs={{8,16},{16,8},{9,17},{17,9},{10,18},{18,10},{11,19},{19,11},{12,20... | collective-permute-start | bytes 2064392 | tf_op jit(solution)/shard_map/ppermute | solution.py:423
  199.4 26.6 %collective-permute-start.29 = (bf16[672,512]{1,0:T(8,128)(2,1)}, bf16[672,512]{1,0:T(8,128)(2,1)}, u32[]{:S(2)}, u32[]{:S(2)}) collective-permute-start(bf16[672,512]{1,0:T(8,128)(2,1)} %get-tuple-element.53), channel_id=1, source_target_pairs={{0,8},{8,0},{16,24},{24,16},{1,9},{9,1},{17,25},{25,17},{2,10},{10... | collective-permute-start | bytes 2064392 | tf_op jit(solution)/shard_map/ppermute | solution.py:423
  217.0 8.9 %collective-permute-start.30 = (bf16[672,512]{1,0:T(8,128)(2,1)S(1)}, bf16[672,512]{1,0:T(8,128)(2,1)}, u32[]{:S(2)}, u32[]{:S(2)}) collective-permute-start(bf16[672,512]{1,0:T(8,128)(2,1)S(1)} %copy-done.8), channel_id=1, source_target_pairs={{8,16},{16,8},{9,17},{17,9},{10,18},{18,10},{11,19},{19,11},{12,20... | collective-permute-start | bytes 2064392 | tf_op jit(solution)/shard_map/ppermute | solution.py:423
  (21 other events, 271.6 us)
Sparse Core Ops, SparseCore 0:
  9.9 44.9 all-gather.1
where the time goes:
time: 241 us; the launch traced here: 239 us
  Pallas kernels  85.8 us (36%)
  waiting for transfers between devices  67 us (28%)
  starting transfers between devices  54.8 us (23%)
  between operations  14.5 us (6%)
  local copies, waits for them, and re-layouts  8.47 us (4%)
  other arithmetic  8.42 us (3%)
    pallas_call x2, Pallas kernels, heads(): pl.pallas_call(functools.partial(head_kernel, share, halves, spots, len(m...  48.2 us
    ppermute x24, waiting for transfers between devices, link(): return lax.ppermute(value, 'dp', pairs)  47.5 us
    ppermute x24, starting transfers between devices, link(): return lax.ppermute(value, 'dp', pairs)  45.9 us
    pallas_call x4, Pallas kernels, token_terms(): pl.pallas_call(functools.partial(token_kernel, len(adds), len(parts), len...  22.4 us
    ppermute x3, waiting for transfers between devices, local(): lax.ppermute(part, 'seq', [(i, i ^ 2 * other) for i in range(owners)])  18.7 us
    pallas_call x5, Pallas kernels, mix(): pl.pallas_call(functools.partial(mix_kernel, outs, len(sources), len(mark...  11.3 us
  transfers between devices with their start and end apart: 33, of which 9 were waited for; matrix products, arithmetic and copies ran while one was open for 6% of the time, Pallas kernels for 35%

commit v1 on v0

--- a/solution.py
+++ b/solution.py
@@ -553,7 +553,7 @@
         outs.append(out)
         outer_cases, inner_cases = exchange_cases(3, 0, 1, 2)
         outer_cases = exchange_cases(1, 3, None, None)[0] + outer_cases[2:]
-        marks = mix((outer_cases, inner_cases), (old, *received, terms), ())
+        marks = mix((outer_cases, inner_cases), (old, *received, terms), (edge_received,))
         received = link(marks[0], *OUTER), link(marks[1], *INNER)
         layout = [
             [(0, 4, 0, True)],
@@ -598,10 +598,11 @@
     )
     layout += whole(planes, len(sources))
     sources += [terms, *received]
+    attn_out = spread.reshape(owners, rows, groups * wide).transpose(1, 0, 2)
+    attn_out = attn_out.reshape(rows, owners * groups * wide)
+    sources[0] = after(sources[0], attn_out)
     weight_grads = total_terms(share, layout, sources)
     token_grad = add(*shares).astype(jnp.bfloat16)
-    attn_out = spread.reshape(owners, rows, groups * wide).transpose(1, 0, 2)
-    attn_out = attn_out.reshape(rows, owners * groups * wide)
     return (attn_out, token_grad, *weight_grads)
 
 

time: 241 us -> 240 us (level)
    all_to_all x1, waiting for transfers between devices: 0.01 us -> 6.09 us  [local(): lax.all_to_all(after(jnp.concatenate(outs, axis=1), *marks), 'seq', split...]
    ppermute x24, waiting for transfers between devices: 47.5 us -> 43.4 us  [link(): return lax.ppermute(value, 'dp', pairs)]
  transfers between devices with their start and end apart: 33 -> 33, of which waited for: 9 -> 9; matrix products, arithmetic and copies ran while one was open for 6% -> 6% of each run, Pallas kernels for 35% -> 33%
where the time goes in v1:
time: 240 us; the launch traced here: 239 us
  Pallas kernels  85.8 us (36%)
  waiting for transfers between devices  67.5 us (28%)
  starting transfers between devices  55.2 us (23%)
  between operations  14.5 us (6%)
  other arithmetic  8.43 us (4%)
  local copies, waits for them, and re-layouts  7.23 us (3%)
    pallas_call x2, Pallas kernels, heads(): pl.pallas_call(functools.partial(head_kernel, share, halves, spots, len(m...  48.2 us
    ppermute x24, starting transfers between devices, link(): return lax.ppermute(value, 'dp', pairs)  46.8 us
    ppermute x24, waiting for transfers between devices, link(): return lax.ppermute(value, 'dp', pairs)  43.4 us
    pallas_call x4, Pallas kernels, token_terms(): pl.pallas_call(functools.partial(token_kernel, len(adds), len(parts), len...  22.4 us
    ppermute x3, waiting for transfers between devices, local(): lax.ppermute(part, 'seq', [(i, i ^ 2 * other) for i in range(owners)])  17.4 us
    pallas_call x5, Pallas kernels, mix(): pl.pallas_call(functools.partial(mix_kernel, outs, len(sources), len(mark...  11.3 us
    all_to_all x1, waiting for transfers between devices, local(): lax.all_to_all(after(jnp.concatenate(outs, axis=1), *marks), 'seq', split...  6.09 us
  transfers between devices with their start and end apart: 33, of which 9 were waited for; matrix products, arithmetic and copies ran while one was open for 6% of the time, Pallas kernels for 33%

profile of v1, /device:TPU:0, one launch (start us, length us, event | category | flops | bytes accessed | tf_op | source)
XLA Modules:
  0.0 238.7 jit_solution(1922883697774384875)
XLA Ops:
  9.2 3.1 %collective-permute-start.5 = (bf16[672,256]{1,0:T(8,128)(2,1)S(1)}, bf16[672,256]{1,0:T(8,128)(2,1)S(1)}, u32[]{:S(2)}, u32[]{:S(2)}) collective-permute-start(bf16[672,256]{1,0:T(8,128)(2,1)S(1)} %pad_maximum_fusion.4.refs_6_), channel_id=1, source_target_pairs={{0,8},{8,0},{16,24},{24,16},{1,9},{9,1},{17,25},{25,17},{2,10},{10... | collective-permute-start | bytes 1032200 | tf_op jit(solution)/shard_map/ppermute | solution.py:423
  13.0 4.4 %collective-permute-start = (bf16[672,256]{1,0:T(8,128)(2,1)S(1)}, bf16[672,256]{1,0:T(8,128)(2,1)S(1)}, u32[]{:S(2)}, u32[]{:S(2)}) collective-permute-start(bf16[672,256]{1,0:T(8,128)(2,1)S(1)} %get-tuple-element.66.refs_0_), channel_id=1, source_target_pairs={{0,8},{8,0},{16,24},{24,16},{1,9},{9,1},{17,25},{25,17},{2,10},{10... | collective-permute-start | bytes 1032200 | tf_op jit(solution)/shard_map/ppermute | solution.py:423
  18.5 2.7 %collective-permute-done.5.refs_7_ = bf16[672,256]{1,0:T(8,128)(2,1)S(1)} collective-permute-done((bf16[672,256]{1,0:T(8,128)(2,1)S(1)}, bf16[672,256]{1,0:T(8,128)(2,1)S(1)}, u32[]{:S(2)}, u32[]{:S(2)}) %collective-permute-start.5) | collective-permute-done | bytes 344096 | tf_op jit(solution)/shard_map/ppermute | solution.py:423
  21.9 5.9 %collective-permute-done.refs_1_ = bf16[672,256]{1,0:T(8,128)(2,1)S(1)} collective-permute-done((bf16[672,256]{1,0:T(8,128)(2,1)S(1)}, bf16[672,256]{1,0:T(8,128)(2,1)S(1)}, u32[]{:S(2)}, u32[]{:S(2)}) %collective-permute-start) | collective-permute-done | bytes 344096 | tf_op jit(solution)/shard_map/ppermute | solution.py:423
  28.4 1.9 fusion.3
  38.9 15.0 %collective-permute-done.3.refs_4_ = bf16[672,256]{1,0:T(8,128)(2,1)S(1)} collective-permute-done((bf16[672,256]{1,0:T(8,128)(2,1)S(1)}, bf16[672,256]{1,0:T(8,128)(2,1)S(1)}, u32[]{:S(2)}, u32[]{:S(2)}) %collective-permute-start.3) | collective-permute-done | bytes 344096 | tf_op jit(solution)/shard_map/ppermute | solution.py:423
  53.9 12.9 %collective-permute-done.4.refs_5_ = bf16[672,256]{1,0:T(8,128)(2,1)S(1)} collective-permute-done((bf16[672,256]{1,0:T(8,128)(2,1)S(1)}, bf16[672,256]{1,0:T(8,128)(2,1)S(1)}, u32[]{:S(2)}, u32[]{:S(2)}) %collective-permute-start.4) | collective-permute-done | bytes 344096 | tf_op jit(solution)/shard_map/ppermute | solution.py:423
  69.2 24.1 %heads.2 = (bf16[1024,256]{1,0:T(8,128)(2,1)}, bf16[1024,512]{1,0:T(8,128)(2,1)}, bf16[2688,512]{1,0:T(8,128)(2,1)}, bf16[2688,512]{1,0:T(8,128)(2,1)}) custom-call(s32[1,4]{1,0:T(1,128)} %lengths_ref.3, f32[1,128]{1,0:T(1,128)} %bitcast.46, f32[1,128]{1,0:T(1,128)} %bitcast.48, bf16[672,256]{1,0:T(8,128)(2,1)} %copy-done.6, bf16[672,256]{1,0:T(8,128)(2,1)} %copy-done.11, ...), custom_call_target="tpu_custom_call" | custom-call | flops 8858370048 | bytes 17956864 | tf_op jit(solution)/shard_map/heads/pallas_call | solution.py:200
  93.3 2.0 mix.5.refs_0_
  95.3 5.7 %collective-permute-start.14 = (bf16[672,512]{1,0:T(8,128)(2,1)}, bf16[672,512]{1,0:T(8,128)(2,1)}, u32[]{:S(2)}, u32[]{:S(2)}) collective-permute-start(bf16[672,512]{1,0:T(8,128)(2,1)} %mix.5.refs_0_), channel_id=1, source_target_pairs={{0,8},{24,16},{1,9},{25,17},{2,10},{26,18},{3,11},{27,19},{4,12},{... | collective-permute-start | bytes 2064392 | tf_op jit(solution)/shard_map/ppermute | solution.py:423
  102.3 4.9 %token_terms.4.refs_2_.refs_0_ = bf16[4,128,2688]{2,1,0:T(8,128)(2,1)} custom-call(s32[1]{0:T(128)} %bitcast.7.side_ref, bf16[4,2,128,512]{3,2,1,0:T(8,128)(2,1)} %bitcast.37, bf16[2688,512]{1,0:T(8,128)(2,1)} %get-tuple-element.38.weight_ref, bf16[672,512]{1,0:T(8,128)(2,1)} %mix.5.refs_0_, bf16[672,512]{1,0:T(8,128)(2,1)} %collective-permute-done.12.refs_1_.refs_3_), custom_call_target="tpu_custom_call" | custom-call | flops 524288 | bytes 524288 | tf_op jit(solution)/shard_map/token_terms/pallas_call | solution.py:275
  107.2 5.6 %collective-permute-done.14.refs_1_ = bf16[672,512]{1,0:T(8,128)(2,1)} collective-permute-done((bf16[672,512]{1,0:T(8,128)(2,1)}, bf16[672,512]{1,0:T(8,128)(2,1)}, u32[]{:S(2)}, u32[]{:S(2)}) %collective-permute-start.14) | collective-permute-done | bytes 688160 | tf_op jit(solution)/shard_map/ppermute | solution.py:423
  112.9 2.7 %mix.6 = (bf16[672,512]{1,0:T(8,128)(2,1)}, bf16[672,512]{1,0:T(8,128)(2,1)}, bf16[672,512]{1,0:T(8,128)(2,1)}) custom-call(bf16[4,672,512]{2,1,0:T(8,128)(2,1)} %bitcast.34, bf16[672,512]{1,0:T(8,128)(2,1)} %collective-permute-done.14.refs_1_, bf16[4,128,2688]{2,1,0:T(8,128)(2,1)} %token_terms.4.refs_2_.refs_0_, ...), custom_call_target="tpu_custom_call" | custom-call | flops 1 | bytes 1 | tf_op jit(solution)/shard_map/mix/pallas_call | solution.py:338
  115.6 5.4 %collective-permute-start.15 = (bf16[672,512]{1,0:T(8,128)(2,1)}, bf16[672,512]{1,0:T(8,128)(2,1)}, u32[]{:S(2)}, u32[]{:S(2)}) collective-permute-start(bf16[672,512]{1,0:T(8,128)(2,1)} %get-tuple-element.39.refs_9_), channel_id=1, source_target_pairs={{0,8},{24,16},{1,9},{25,17},{2,10},{26,18},{3,11},{27,19},{4,12},{... | collective-permute-start | bytes 2064392 | tf_op jit(solution)/shard_map/ppermute | solution.py:423
  121.0 1.6 collective-permute-start.16
  122.5 2.7 %collective-permute-start.17 = (bf16[672,512]{1,0:T(8,128)(2,1)}, bf16[672,512]{1,0:T(8,128)(2,1)}, u32[]{:S(2)}, u32[]{:S(2)}) collective-permute-start(bf16[672,512]{1,0:T(8,128)(2,1)} %get-tuple-element.41.refs_11_), channel_id=1, source_target_pairs={{0,8},{24,16},{1,9},{25,17},{2,10},{26,18},{3,11},{27,19},{4,12},{... | collective-permute-start | bytes 2064392 | tf_op jit(solution)/shard_map/ppermute | solution.py:423
  125.3 24.1 %heads.3 = (bf16[1024,256]{1,0:T(8,128)(2,1)}, bf16[1024,512]{1,0:T(8,128)(2,1)}, bf16[2688,512]{1,0:T(8,128)(2,1)}, bf16[2688,512]{1,0:T(8,128)(2,1)}) custom-call(s32[1,4]{1,0:T(1,128)} %lengths_ref.3, f32[1,128]{1,0:T(1,128)} %bitcast.47, f32[1,128]{1,0:T(1,128)} %bitcast.49, bf16[672,512]{1,0:T(8,128)(2,1)} %pad_maximum_fusion.1.refs_0_, ...), custom_call_target="tpu_custom_call" | custom-call | flops 8858370048 | bytes 17956864 | tf_op jit(solution)/shard_map/heads/pallas_call | solution.py:200
  149.4 2.2 mix.7
  152.2 6.0 %token_terms.5 = (bf16[128,2688]{1,0:T(8,128)(2,1)}, bf16[128,2688]{1,0:T(8,128)(2,1)}, bf16[128,2688]{1,0:T(8,128)(2,1)}, bf16[128,2688]{1,0:T(8,128)(2,1)}) custom-call(s32[1]{0:T(128)} %bitcast.7.side_ref, bf16[4,2,128,512]{3,2,1,0:T(8,128)(2,1)} %bitcast.41, bf16[2688,512]{1,0:T(8,128)(2,1)} %get-tuple-element.46.weight_ref, ...), custom_call_target="tpu_custom_call" | custom-call | flops 524288 | bytes 524288 | tf_op jit(solution)/shard_map/token_terms/pallas_call | solution.py:275
  159.3 4.9 %token_terms.6.refs_2_.refs_0_ = bf16[4,128,2688]{2,1,0:T(8,128)(2,1)} custom-call(s32[1]{0:T(128)} %bitcast.10.side_ref, bf16[4,2,128,512]{3,2,1,0:T(8,128)(2,1)} %bitcast.38, bf16[2688,512]{1,0:T(8,128)(2,1)} %get-tuple-element.38.weight_ref, bf16[128,2688]{1,0:T(8,128)(2,1)} %get-tuple-element.48.refs_0_, bf16[128,2688]{1,0:T(8,128)(2,1)} %get-tuple-element.49.refs_1_, ...), custom_call_target="tpu_custom_call" | custom-call | flops 524288 | bytes 524288 | tf_op jit(solution)/shard_map/token_terms/pallas_call | solution.py:275
  165.4 2.2 mix.8
  167.7 3.7 %collective-permute-start.19 = (bf16[672,512]{1,0:T(8,128)(2,1)}, bf16[672,512]{1,0:T(8,128)(2,1)}, u32[]{:S(2)}, u32[]{:S(2)}) collective-permute-start(bf16[672,512]{1,0:T(8,128)(2,1)} %get-tuple-element.52.refs_5_), channel_id=1, source_target_pairs={{0,8},{24,16},{1,9},{25,17},{2,10},{26,18},{3,11},{27,19},{4,12},{... | collective-permute-start | bytes 2064392 | tf_op jit(solution)/shard_map/ppermute | solution.py:423
  172.9 6.6 %token_terms.7.refs_3_ = bf16[4,128,2688]{2,1,0:T(8,128)(2,1)} custom-call(s32[1]{0:T(128)} %bitcast.10.side_ref, bf16[4,2,128,512]{3,2,1,0:T(8,128)(2,1)} %bitcast.42, bf16[2688,512]{1,0:T(8,128)(2,1)} %get-tuple-element.46.weight_ref, bf16[4,128,2688]{2,1,0:T(8,128)(2,1)} %token_terms.6.refs_2_.refs_0_, bf16[128,2688]{1,0:T(8,128)(2,1)} %collective-permute-done.21.refs_1_, ...), custom_call_target="tpu_custom_call" | custom-call | flops 524288 | bytes 524288 | tf_op jit(solution)/shard_map/token_terms/pallas_call | solution.py:275
  179.5 3.0 %dynamic-slice_bitcast_fusion.2 = (bf16[128,2688]{1,0:T(8,128)(2,1)}, bf16[128,2688]{1,0:T(8,128)(2,1)}, bf16[128,2688]{1,0:T(8,128)(2,1)}) fusion(bf16[4,128,2688]{2,1,0:T(8,128)(2,1)} %token_terms.7.refs_3_, s32[]{:T(128)S(6)} %select_n.19, s32[]{:T(128)S(6)} %select_n.21, s32[]{:T(128)S(6)} %select_n.20), kind=kLoop, calls=%fused_computation.10 | loop fusion | bytes 4128780 | tf_op jit(solution)/shard_map/jit(dynamic_index_in_dim)/squeeze | solution.py:587
  187.0 2.2 mix.9
  189.3 3.9 %all-to-all-start = ((bf16[8,128,512]{2,1,0:T(8,128)(2,1)}), bf16[8,128,512]{2,1,0:T(8,128)(2,1)S(1)}, u32[]{:S(2)}, u32[]{:S(2)}) async-start(bf16[8,128,512]{2,1,0:T(8,128)(2,1)} %bitcast.39), calls=%async_computation | async-start | bytes 2097152 | tf_op jit(solution)/shard_map/all_to_all | solution.py:592
  194.7 4.3 %collective-permute-start.29 = (bf16[672,512]{1,0:T(8,128)(2,1)S(1)}, bf16[672,512]{1,0:T(8,128)(2,1)}, u32[]{:S(2)}, u32[]{:S(2)}) collective-permute-start(bf16[672,512]{1,0:T(8,128)(2,1)S(1)} %copy-done.8), channel_id=1, source_target_pairs={{0,8},{8,0},{16,24},{24,16},{1,9},{9,1},{17,25},{25,17},{2,10},{10... | collective-permute-start | bytes 2064392 | tf_op jit(solution)/shard_map/ppermute | solution.py:423
  198.9 2.2 collective-permute-done.25
  202.6 15.2 %collective-permute-done.26 = bf16[128,2688]{1,0:T(8,128)(2,1)} collective-permute-done((bf16[128,2688]{1,0:T(8,128)(2,1)}, bf16[128,2688]{1,0:T(8,128)(2,1)}, u32[]{:S(2)}, u32[]{:S(2)}) %collective-permute-start.26) | collective-permute-done | bytes 688160 | tf_op jit(solution)/shard_map/ppermute | solution.py:588
  217.8 2.9 %fusion.2 = bf16[128,2688]{1,0:T(8,128)(2,1)} fusion(bf16[128,2688]{1,0:T(8,128)(2,1)} %collective-permute-done.27, bf16[128,2688]{1,0:T(8,128)(2,1)} %collective-permute-done.26, bf16[128,2688]{1,0:T(8,128)(2,1)} %collective-permute-done.25, bf16[4,128,2688]{2,1,0:T(8,128)(2,1)} %token_terms.7.refs_3_, s32[]{:T(128)S(6)} %select_n.18), kind=kLoop, calls=%fused_computation.3 | loop fusion | flops 2752512 | bytes 3440644 | tf_op jit(solution)/shard_map/convert_element_type | solution.py:605
  220.7 6.1 %all-to-all-done = bf16[8,128,512]{2,1,0:T(8,128)(2,1)S(1)} async-done(((bf16[8,128,512]{2,1,0:T(8,128)(2,1)}), bf16[8,128,512]{2,1,0:T(8,128)(2,1)S(1)}, u32[]{:S(2)}, u32[]{:S(2)}) %all-to-all-start) | async-done | bytes 1048608 | tf_op jit(solution)/shard_map/all_to_all | solution.py:592
  227.9 3.9 %total_terms.1 = (f32[672,512]{1,0:T(8,128)}, f32[672,256]{1,0:T(8,128)}, f32[672,256]{1,0:T(8,128)}) custom-call(bf16[4,672,512]{2,1,0:T(8,128)(2,1)} %bitcast.36, bf16[672,512]{1,0:T(8,128)(2,1)} %collective-permute-done.17.refs_4_.refs_1_, bf16[672,512]{1,0:T(8,128)(2,1)} %collective-permute-done.18.refs_1_.refs_2_, ...), custom_call_target="tpu_custom_call" | custom-call | flops 1 | bytes 1 | tf_op jit(solution)/shard_map/total_terms/pallas_call | solution.py:390
  (103 shorter events, 30.3 us)
Async XLA Ops:
  7.2 61.2 %all-gather.2.cloned.1.call-start = ((), (), s32[]{:S(2)}) async-start(), calls=%async_computation.1 | async-start | bytes 6193152 | tf_op jit(solution)/shard_map/all_gather | solution.py:497
  9.2 12.0 %collective-permute-start.5 = (bf16[672,256]{1,0:T(8,128)(2,1)S(1)}, bf16[672,256]{1,0:T(8,128)(2,1)S(1)}, u32[]{:S(2)}, u32[]{:S(2)}) collective-permute-start(bf16[672,256]{1,0:T(8,128)(2,1)S(1)} %pad_maximum_fusion.4.refs_6_), channel_id=1, source_target_pairs={{0,8},{8,0},{16,24},{24,16},{1,9},{9,1},{17,25},{25,17},{2,10},{10... | collective-permute-start | bytes 1032200 | tf_op jit(solution)/shard_map/ppermute | solution.py:423
  12.3 19.4 %collective-permute-start.6 = (bf16[672,256]{1,0:T(8,128)(2,1)S(1)}, bf16[672,256]{1,0:T(8,128)(2,1)S(1)}, u32[]{:S(2)}, u32[]{:S(2)}) collective-permute-start(bf16[672,256]{1,0:T(8,128)(2,1)S(1)} %pad_maximum_fusion.4.refs_6_), channel_id=1, source_target_pairs={{8,16},{16,8},{9,17},{17,9},{10,18},{18,10},{11,19},{19,11},{12,20... | collective-permute-start | bytes 1032200 | tf_op jit(solution)/shard_map/ppermute | solution.py:423
  13.0 14.7 %collective-permute-start = (bf16[672,256]{1,0:T(8,128)(2,1)S(1)}, bf16[672,256]{1,0:T(8,128)(2,1)S(1)}, u32[]{:S(2)}, u32[]{:S(2)}) collective-permute-start(bf16[672,256]{1,0:T(8,128)(2,1)S(1)} %get-tuple-element.66.refs_0_), channel_id=1, source_target_pairs={{0,8},{8,0},{16,24},{24,16},{1,9},{9,1},{17,25},{25,17},{2,10},{10... | collective-permute-start | bytes 1032200 | tf_op jit(solution)/shard_map/ppermute | solution.py:423
  17.5 15.5 %collective-permute-start.1 = (bf16[672,256]{1,0:T(8,128)(2,1)S(1)}, bf16[672,256]{1,0:T(8,128)(2,1)S(1)}, u32[]{:S(2)}, u32[]{:S(2)}) collective-permute-start(bf16[672,256]{1,0:T(8,128)(2,1)S(1)} %get-tuple-element.66.refs_0_), channel_id=1, source_target_pairs={{8,16},{16,8},{9,17},{17,9},{10,18},{18,10},{11,19},{19,11},{12,20... | collective-permute-start | bytes 1032200 | tf_op jit(solution)/shard_map/ppermute | solution.py:423
  21.2 13.1 %collective-permute-start.7 = (bf16[672,256]{1,0:T(8,128)(2,1)S(1)}, bf16[672,256]{1,0:T(8,128)(2,1)S(1)}, u32[]{:S(2)}, u32[]{:S(2)}) collective-permute-start(bf16[672,256]{1,0:T(8,128)(2,1)S(1)} %collective-permute-done.5.refs_7_), channel_id=1, source_target_pairs={{8,16},{16,8},{9,17},{17,9},{10,18},{18,10},{11,19},{19,11},{12,20... | collective-permute-start | bytes 1032200 | tf_op jit(solution)/shard_map/ppermute | solution.py:423
  31.7 36.6 %collective-permute-start.8 = (bf16[672,256]{1,0:T(8,128)(2,1)S(1)}, bf16[672,256]{1,0:T(8,128)(2,1)S(1)}, u32[]{:S(2)}, u32[]{:S(2)}) collective-permute-start(bf16[672,256]{1,0:T(8,128)(2,1)S(1)} %collective-permute-done.6.refs_8_), channel_id=1, source_target_pairs={{8,0},{16,24},{9,1},{17,25},{10,2},{18,26},{11,3},{19,27},{12,4},{... | collective-permute-start | bytes 1032200 | tf_op jit(solution)/shard_map/ppermute | solution.py:423
  33.0 20.8 %collective-permute-start.3 = (bf16[672,256]{1,0:T(8,128)(2,1)S(1)}, bf16[672,256]{1,0:T(8,128)(2,1)S(1)}, u32[]{:S(2)}, u32[]{:S(2)}) collective-permute-start(bf16[672,256]{1,0:T(8,128)(2,1)S(1)} %collective-permute-done.1.refs_2_), channel_id=1, source_target_pairs={{8,0},{16,24},{9,1},{17,25},{10,2},{18,26},{11,3},{19,27},{12,4},{... | collective-permute-start | bytes 1032200 | tf_op jit(solution)/shard_map/ppermute | solution.py:423
  34.3 34.0 %collective-permute-start.9 = (bf16[672,256]{1,0:T(8,128)(2,1)S(1)}, bf16[672,256]{1,0:T(8,128)(2,1)S(1)}, u32[]{:S(2)}, u32[]{:S(2)}) collective-permute-start(bf16[672,256]{1,0:T(8,128)(2,1)S(1)} %collective-permute-done.7.refs_9_), channel_id=1, source_target_pairs={{8,0},{16,24},{9,1},{17,25},{10,2},{18,26},{11,3},{19,27},{12,4},{... | collective-permute-start | bytes 1032200 | tf_op jit(solution)/shard_map/ppermute | solution.py:423
  35.7 31.1 %collective-permute-start.4 = (bf16[672,256]{1,0:T(8,128)(2,1)S(1)}, bf16[672,256]{1,0:T(8,128)(2,1)S(1)}, u32[]{:S(2)}, u32[]{:S(2)}) collective-permute-start(bf16[672,256]{1,0:T(8,128)(2,1)S(1)} %collective-permute-done.2.refs_3_), channel_id=1, source_target_pairs={{8,0},{16,24},{9,1},{17,25},{10,2},{18,26},{11,3},{19,27},{12,4},{... | collective-permute-start | bytes 1032200 | tf_op jit(solution)/shard_map/ppermute | solution.py:423
  53.9 47.2 %collective-permute-start.12 = (bf16[672,512]{1,0:T(8,128)(2,1)}, bf16[672,512]{1,0:T(8,128)(2,1)}, u32[]{:S(2)}, u32[]{:S(2)}) collective-permute-start(bf16[672,512]{1,0:T(8,128)(2,1)} %pad_maximum_fusion.1.refs_0_), channel_id=1, source_target_pairs={{0,16},{8,24},{16,0},{24,8},{1,17},{9,25},{17,1},{25,9},{2,18},{10... | collective-permute-start | bytes 2064392 | tf_op jit(solution)/shard_map/ppermute | solution.py:423
  66.7 40.5 %collective-permute-start.10 = (bf16[672,512]{1,0:T(8,128)(2,1)}, bf16[672,512]{1,0:T(8,128)(2,1)}, u32[]{:S(2)}, u32[]{:S(2)}) collective-permute-start(bf16[672,512]{1,0:T(8,128)(2,1)} %pad_maximum_fusion.1.refs_0_), channel_id=1, source_target_pairs={{0,8},{8,0},{16,24},{24,16},{1,9},{9,1},{17,25},{25,17},{2,10},{10... | collective-permute-start | bytes 2064392 | tf_op jit(solution)/shard_map/ppermute | solution.py:423
  66.8 40.5 %collective-permute-start.11 = (bf16[672,512]{1,0:T(8,128)(2,1)}, bf16[672,512]{1,0:T(8,128)(2,1)}, u32[]{:S(2)}, u32[]{:S(2)}) collective-permute-start(bf16[672,512]{1,0:T(8,128)(2,1)} %pad_maximum_fusion.1.refs_0_), channel_id=1, source_target_pairs={{8,16},{16,8},{9,17},{17,9},{10,18},{18,10},{11,19},{19,11},{12,20... | collective-permute-start | bytes 2064392 | tf_op jit(solution)/shard_map/ppermute | solution.py:423
  95.3 17.6 %collective-permute-start.14 = (bf16[672,512]{1,0:T(8,128)(2,1)}, bf16[672,512]{1,0:T(8,128)(2,1)}, u32[]{:S(2)}, u32[]{:S(2)}) collective-permute-start(bf16[672,512]{1,0:T(8,128)(2,1)} %mix.5.refs_0_), channel_id=1, source_target_pairs={{0,8},{24,16},{1,9},{25,17},{2,10},{26,18},{3,11},{27,19},{4,12},{... | collective-permute-start | bytes 2064392 | tf_op jit(solution)/shard_map/ppermute | solution.py:423
  101.0 24.3 %collective-permute-start.13 = (bf16[672,512]{1,0:T(8,128)(2,1)}, bf16[672,512]{1,0:T(8,128)(2,1)}, u32[]{:S(2)}, u32[]{:S(2)}) collective-permute-start(bf16[672,512]{1,0:T(8,128)(2,1)} %collective-permute-done.12.refs_1_.refs_3_), channel_id=1, source_target_pairs={{8,0},{16,24},{9,1},{17,25},{10,2},{18,26},{11,3},{19,27},{12,4},{... | collective-permute-start | bytes 2064392 | tf_op jit(solution)/shard_map/ppermute | solution.py:423
  115.6 33.8 %collective-permute-start.15 = (bf16[672,512]{1,0:T(8,128)(2,1)}, bf16[672,512]{1,0:T(8,128)(2,1)}, u32[]{:S(2)}, u32[]{:S(2)}) collective-permute-start(bf16[672,512]{1,0:T(8,128)(2,1)} %get-tuple-element.39.refs_9_), channel_id=1, source_target_pairs={{0,8},{24,16},{1,9},{25,17},{2,10},{26,18},{3,11},{27,19},{4,12},{... | collective-permute-start | bytes 2064392 | tf_op jit(solution)/shard_map/ppermute | solution.py:423
  121.0 28.4 %collective-permute-start.16 = (bf16[672,512]{1,0:T(8,128)(2,1)}, bf16[672,512]{1,0:T(8,128)(2,1)}, u32[]{:S(2)}, u32[]{:S(2)}) collective-permute-start(bf16[672,512]{1,0:T(8,128)(2,1)} %get-tuple-element.40.refs_10_), channel_id=1, source_target_pairs={{8,16},{16,8},{9,17},{17,9},{10,18},{18,10},{11,19},{19,11},{12,20... | collective-permute-start | bytes 2064392 | tf_op jit(solution)/shard_map/ppermute | solution.py:423
  122.5 26.8 %collective-permute-start.17 = (bf16[672,512]{1,0:T(8,128)(2,1)}, bf16[672,512]{1,0:T(8,128)(2,1)}, u32[]{:S(2)}, u32[]{:S(2)}) collective-permute-start(bf16[672,512]{1,0:T(8,128)(2,1)} %get-tuple-element.41.refs_11_), channel_id=1, source_target_pairs={{0,8},{24,16},{1,9},{25,17},{2,10},{26,18},{3,11},{27,19},{4,12},{... | collective-permute-start | bytes 2064392 | tf_op jit(solution)/shard_map/ppermute | solution.py:423
  151.6 13.8 %collective-permute-start.18 = (bf16[672,512]{1,0:T(8,128)(2,1)}, bf16[672,512]{1,0:T(8,128)(2,1)}, u32[]{:S(2)}, u32[]{:S(2)}) collective-permute-start(bf16[672,512]{1,0:T(8,128)(2,1)} %get-tuple-element.44.refs_1_), channel_id=1, source_target_pairs={{0,8},{8,0},{16,24},{24,16},{1,9},{9,1},{17,25},{25,17},{2,10},{10... | collective-permute-start | bytes 2064392 | tf_op jit(solution)/shard_map/ppermute | solution.py:423
  158.3 13.1 %collective-permute-start.21 = (bf16[128,2688]{1,0:T(8,128)(2,1)}, bf16[128,2688]{1,0:T(8,128)(2,1)}, u32[]{:S(2)}, u32[]{:S(2)}) collective-permute-start(bf16[128,2688]{1,0:T(8,128)(2,1)} %get-tuple-element.48.refs_0_), channel_id=1, source_target_pairs={{0,1},{1,0},{2,3},{3,2},{4,5},{5,4},{6,7},{7,6},{8,9},{9,8},{10,11... | collective-permute-start | bytes 2064392 | tf_op jit(solution)/shard_map/ppermute | solution.py:578
  158.3 14.6 %collective-permute-start.22 = (bf16[128,2688]{1,0:T(8,128)(2,1)}, bf16[128,2688]{1,0:T(8,128)(2,1)}, u32[]{:S(2)}, u32[]{:S(2)}) collective-permute-start(bf16[128,2688]{1,0:T(8,128)(2,1)} %get-tuple-element.49.refs_1_), channel_id=1, source_target_pairs={{0,1},{1,0},{2,3},{3,2},{4,5},{5,4},{6,7},{7,6},{8,9},{9,8},{10,11... | collective-permute-start | bytes 2064392 | tf_op jit(solution)/shard_map/ppermute | solution.py:578
  158.8 14.1 %collective-permute-start.23 = (bf16[128,2688]{1,0:T(8,128)(2,1)}, bf16[128,2688]{1,0:T(8,128)(2,1)}, u32[]{:S(2)}, u32[]{:S(2)}) collective-permute-start(bf16[128,2688]{1,0:T(8,128)(2,1)} %get-tuple-element.50.refs_2_), channel_id=1, source_target_pairs={{0,1},{1,0},{2,3},{3,2},{4,5},{5,4},{6,7},{7,6},{8,9},{9,8},{10,11... | collective-permute-start | bytes 2064392 | tf_op jit(solution)/shard_map/ppermute | solution.py:578
  158.8 14.1 %collective-permute-start.24 = (bf16[128,2688]{1,0:T(8,128)(2,1)}, bf16[128,2688]{1,0:T(8,128)(2,1)}, u32[]{:S(2)}, u32[]{:S(2)}) collective-permute-start(bf16[128,2688]{1,0:T(8,128)(2,1)} %get-tuple-element.51.refs_3_), channel_id=1, source_target_pairs={{0,1},{1,0},{2,3},{3,2},{4,5},{5,4},{6,7},{7,6},{8,9},{9,8},{10,11... | collective-permute-start | bytes 2064392 | tf_op jit(solution)/shard_map/ppermute | solution.py:578
  167.7 19.3 %collective-permute-start.19 = (bf16[672,512]{1,0:T(8,128)(2,1)}, bf16[672,512]{1,0:T(8,128)(2,1)}, u32[]{:S(2)}, u32[]{:S(2)}) collective-permute-start(bf16[672,512]{1,0:T(8,128)(2,1)} %get-tuple-element.52.refs_5_), channel_id=1, source_target_pairs={{0,8},{24,16},{1,9},{25,17},{2,10},{26,18},{3,11},{27,19},{4,12},{... | collective-permute-start | bytes 2064392 | tf_op jit(solution)/shard_map/ppermute | solution.py:423
  171.4 15.6 %collective-permute-start.20 = (bf16[672,512]{1,0:T(8,128)(2,1)}, bf16[672,512]{1,0:T(8,128)(2,1)}, u32[]{:S(2)}, u32[]{:S(2)}) collective-permute-start(bf16[672,512]{1,0:T(8,128)(2,1)} %get-tuple-element.53.refs_6_), channel_id=1, source_target_pairs={{8,16},{16,8},{9,17},{17,9},{10,18},{18,10},{11,19},{19,11},{12,20... | collective-permute-start | bytes 2064392 | tf_op jit(solution)/shard_map/ppermute | solution.py:423
  182.4 18.7 %collective-permute-start.25 = (bf16[128,2688]{1,0:T(8,128)(2,1)}, bf16[128,2688]{1,0:T(8,128)(2,1)}, u32[]{:S(2)}, u32[]{:S(2)}) collective-permute-start(bf16[128,2688]{1,0:T(8,128)(2,1)} %get-tuple-element.61), channel_id=1, source_target_pairs={{0,2},{1,3},{2,0},{3,1},{4,6},{5,7},{6,4},{7,5},{8,10},{9,11},{10,... | collective-permute-start | bytes 2064392 | tf_op jit(solution)/shard_map/ppermute | solution.py:588
  183.9 33.9 %collective-permute-start.26 = (bf16[128,2688]{1,0:T(8,128)(2,1)}, bf16[128,2688]{1,0:T(8,128)(2,1)}, u32[]{:S(2)}, u32[]{:S(2)}) collective-permute-start(bf16[128,2688]{1,0:T(8,128)(2,1)} %get-tuple-element.63), channel_id=1, source_target_pairs={{0,4},{1,5},{2,6},{3,7},{4,0},{5,1},{6,2},{7,3},{8,12},{9,13},{10,... | collective-permute-start | bytes 2064392 | tf_op jit(solution)/shard_map/ppermute | solution.py:588
  185.4 32.4 %collective-permute-start.27 = (bf16[128,2688]{1,0:T(8,128)(2,1)}, bf16[128,2688]{1,0:T(8,128)(2,1)}, u32[]{:S(2)}, u32[]{:S(2)}) collective-permute-start(bf16[128,2688]{1,0:T(8,128)(2,1)} %get-tuple-element.62), channel_id=1, source_target_pairs={{0,6},{1,7},{2,4},{3,5},{4,2},{5,3},{6,0},{7,1},{8,14},{9,15},{10,... | collective-permute-start | bytes 2064392 | tf_op jit(solution)/shard_map/ppermute | solution.py:588
  189.3 37.6 %all-to-all-start = ((bf16[8,128,512]{2,1,0:T(8,128)(2,1)}), bf16[8,128,512]{2,1,0:T(8,128)(2,1)S(1)}, u32[]{:S(2)}, u32[]{:S(2)}) async-start(bf16[8,128,512]{2,1,0:T(8,128)(2,1)} %bitcast.39), calls=%async_computation | async-start | bytes 2097152 | tf_op jit(solution)/shard_map/all_to_all | solution.py:592
  193.1 34.8 %collective-permute-start.28 = (bf16[672,512]{1,0:T(8,128)(2,1)S(1)}, bf16[672,512]{1,0:T(8,128)(2,1)}, u32[]{:S(2)}, u32[]{:S(2)}) collective-permute-start(bf16[672,512]{1,0:T(8,128)(2,1)S(1)} %copy-done.2), channel_id=1, source_target_pairs={{8,16},{16,8},{9,17},{17,9},{10,18},{18,10},{11,19},{19,11},{12,20... | collective-permute-start | bytes 2064392 | tf_op jit(solution)/shard_map/ppermute | solution.py:423
  194.7 33.2 %collective-permute-start.29 = (bf16[672,512]{1,0:T(8,128)(2,1)S(1)}, bf16[672,512]{1,0:T(8,128)(2,1)}, u32[]{:S(2)}, u32[]{:S(2)}) collective-permute-start(bf16[672,512]{1,0:T(8,128)(2,1)S(1)} %copy-done.8), channel_id=1, source_target_pairs={{0,8},{8,0},{16,24},{24,16},{1,9},{9,1},{17,25},{25,17},{2,10},{10... | collective-permute-start | bytes 2064392 | tf_op jit(solution)/shard_map/ppermute | solution.py:423
  201.1 26.8 %collective-permute-start.30 = (bf16[672,512]{1,0:T(8,128)(2,1)S(1)}, bf16[672,512]{1,0:T(8,128)(2,1)}, u32[]{:S(2)}, u32[]{:S(2)}) collective-permute-start(bf16[672,512]{1,0:T(8,128)(2,1)S(1)} %copy-done.7), channel_id=1, source_target_pairs={{8,16},{16,8},{9,17},{17,9},{10,18},{18,10},{11,19},{19,11},{12,20... | collective-permute-start | bytes 2064392 | tf_op jit(solution)/shard_map/ppermute | solution.py:423
  (21 other events, 249.6 us)
Sparse Core Ops, SparseCore 0:
  9.9 44.9 all-gather.1

commit v2 on v1

--- a/solution.py
+++ b/solution.py
@@ -527,8 +527,9 @@
         pieces, spots = gather_four(halves(0))
         block = after(jnp.concatenate(halves(1), axis=1), pieces[4])
         far = link(block, (0, 2), (1, 3), (2, 0), (3, 1))
+        middle = link(block, *INNER)
         block = after(block, pieces[5])
-        near, middle = link(block, *OUTER), link(block, *INNER)
+        near = link(block, *OUTER)
         out, grad, weight, terms = group_heads(0, pieces, spots, parts=2)
         outs.append(out)
         (first,) = mix((exchange_cases(1, 0, None, None)[0],), (terms,), ())

time: 240 us -> 237 us (0.988)
  transfers between devices with their start and end apart: 33 -> 33, of which waited for: 9 -> 9; matrix products, arithmetic and copies ran while one was open for 6% -> 6% of each run, Pallas kernels for 33% -> 34%
where the time goes in v2:
time: 237 us; the launch traced here: 236 us
  Pallas kernels  85.9 us (36%)
  waiting for transfers between devices  66 us (28%)
  starting transfers between devices  53.7 us (23%)
  between operations  14.5 us (6%)
  other arithmetic  8.43 us (4%)
  local copies, waits for them, and re-layouts  7.29 us (3%)
    pallas_call x2, Pallas kernels, heads(): pl.pallas_call(functools.partial(head_kernel, share, halves, spots, len(m...  48.2 us
    ppermute x24, starting transfers between devices, link(): return lax.ppermute(value, 'dp', pairs)  45.3 us
    ppermute x24, waiting for transfers between devices, link(): return lax.ppermute(value, 'dp', pairs)  42 us
    pallas_call x4, Pallas kernels, token_terms(): pl.pallas_call(functools.partial(token_kernel, len(adds), len(parts), len...  22.4 us
    ppermute x3, waiting for transfers between devices, local(): lax.ppermute(part, 'seq', [(i, i ^ 2 * other) for i in range(owners)])  18.7 us
    pallas_call x5, Pallas kernels, mix(): pl.pallas_call(functools.partial(mix_kernel, outs, len(sources), len(mark...  11.3 us
  transfers between devices with their start and end apart: 33, of which 9 were waited for; matrix products, arithmetic and copies ran while one was open for 6% of the time, Pallas kernels for 34%

profile of v2, /device:TPU:0, one launch (start us, length us, event | category | flops | bytes accessed | tf_op | source)
XLA Modules:
  0.0 235.8 jit_solution(17481171690308529500)
XLA Ops:
  9.2 3.1 %collective-permute-start.5 = (bf16[672,256]{1,0:T(8,128)(2,1)S(1)}, bf16[672,256]{1,0:T(8,128)(2,1)S(1)}, u32[]{:S(2)}, u32[]{:S(2)}) collective-permute-start(bf16[672,256]{1,0:T(8,128)(2,1)S(1)} %pad_maximum_fusion.4.refs_6_), channel_id=1, source_target_pairs={{0,8},{8,0},{16,24},{24,16},{1,9},{9,1},{17,25},{25,17},{2,10},{10... | collective-permute-start | bytes 1032200 | tf_op jit(solution)/shard_map/ppermute | solution.py:423
  13.0 4.4 %collective-permute-start = (bf16[672,256]{1,0:T(8,128)(2,1)S(1)}, bf16[672,256]{1,0:T(8,128)(2,1)S(1)}, u32[]{:S(2)}, u32[]{:S(2)}) collective-permute-start(bf16[672,256]{1,0:T(8,128)(2,1)S(1)} %get-tuple-element.66.refs_0_), channel_id=1, source_target_pairs={{0,8},{8,0},{16,24},{24,16},{1,9},{9,1},{17,25},{25,17},{2,10},{10... | collective-permute-start | bytes 1032200 | tf_op jit(solution)/shard_map/ppermute | solution.py:423
  18.5 2.7 %collective-permute-done.5.refs_7_ = bf16[672,256]{1,0:T(8,128)(2,1)S(1)} collective-permute-done((bf16[672,256]{1,0:T(8,128)(2,1)S(1)}, bf16[672,256]{1,0:T(8,128)(2,1)S(1)}, u32[]{:S(2)}, u32[]{:S(2)}) %collective-permute-start.5) | collective-permute-done | bytes 344096 | tf_op jit(solution)/shard_map/ppermute | solution.py:423
  21.9 5.9 %collective-permute-done.refs_1_ = bf16[672,256]{1,0:T(8,128)(2,1)S(1)} collective-permute-done((bf16[672,256]{1,0:T(8,128)(2,1)S(1)}, bf16[672,256]{1,0:T(8,128)(2,1)S(1)}, u32[]{:S(2)}, u32[]{:S(2)}) %collective-permute-start) | collective-permute-done | bytes 344096 | tf_op jit(solution)/shard_map/ppermute | solution.py:423
  28.4 1.9 fusion.3
  38.9 15.0 %collective-permute-done.3.refs_4_ = bf16[672,256]{1,0:T(8,128)(2,1)S(1)} collective-permute-done((bf16[672,256]{1,0:T(8,128)(2,1)S(1)}, bf16[672,256]{1,0:T(8,128)(2,1)S(1)}, u32[]{:S(2)}, u32[]{:S(2)}) %collective-permute-start.3) | collective-permute-done | bytes 344096 | tf_op jit(solution)/shard_map/ppermute | solution.py:423
  55.4 11.4 %collective-permute-done.4.refs_5_ = bf16[672,256]{1,0:T(8,128)(2,1)S(1)} collective-permute-done((bf16[672,256]{1,0:T(8,128)(2,1)S(1)}, bf16[672,256]{1,0:T(8,128)(2,1)S(1)}, u32[]{:S(2)}, u32[]{:S(2)}) %collective-permute-start.4) | collective-permute-done | bytes 344096 | tf_op jit(solution)/shard_map/ppermute | solution.py:423
  67.7 24.1 %heads.2 = (bf16[1024,256]{1,0:T(8,128)(2,1)}, bf16[1024,512]{1,0:T(8,128)(2,1)}, bf16[2688,512]{1,0:T(8,128)(2,1)}, bf16[2688,512]{1,0:T(8,128)(2,1)}) custom-call(s32[1,4]{1,0:T(1,128)} %lengths_ref.3, f32[1,128]{1,0:T(1,128)} %bitcast.46, f32[1,128]{1,0:T(1,128)} %bitcast.48, bf16[672,256]{1,0:T(8,128)(2,1)} %copy-done.6, bf16[672,256]{1,0:T(8,128)(2,1)} %copy-done.11, ...), custom_call_target="tpu_custom_call" | custom-call | flops 8858370048 | bytes 17956864 | tf_op jit(solution)/shard_map/heads/pallas_call | solution.py:200
  91.9 2.0 mix.5.refs_0_
  93.9 4.1 %collective-permute-start.14 = (bf16[672,512]{1,0:T(8,128)(2,1)}, bf16[672,512]{1,0:T(8,128)(2,1)}, u32[]{:S(2)}, u32[]{:S(2)}) collective-permute-start(bf16[672,512]{1,0:T(8,128)(2,1)} %mix.5.refs_0_), channel_id=1, source_target_pairs={{0,8},{24,16},{1,9},{25,17},{2,10},{26,18},{3,11},{27,19},{4,12},{... | collective-permute-start | bytes 2064392 | tf_op jit(solution)/shard_map/ppermute | solution.py:423
  99.3 4.9 %token_terms.4.refs_2_.refs_0_ = bf16[4,128,2688]{2,1,0:T(8,128)(2,1)} custom-call(s32[1]{0:T(128)} %bitcast.7.side_ref, bf16[4,2,128,512]{3,2,1,0:T(8,128)(2,1)} %bitcast.37, bf16[2688,512]{1,0:T(8,128)(2,1)} %get-tuple-element.38.weight_ref, bf16[672,512]{1,0:T(8,128)(2,1)} %mix.5.refs_0_, bf16[672,512]{1,0:T(8,128)(2,1)} %collective-permute-done.12.refs_1_.refs_3_), custom_call_target="tpu_custom_call" | custom-call | flops 524288 | bytes 524288 | tf_op jit(solution)/shard_map/token_terms/pallas_call | solution.py:275
  104.2 6.0 %collective-permute-done.14.refs_1_ = bf16[672,512]{1,0:T(8,128)(2,1)} collective-permute-done((bf16[672,512]{1,0:T(8,128)(2,1)}, bf16[672,512]{1,0:T(8,128)(2,1)}, u32[]{:S(2)}, u32[]{:S(2)}) %collective-permute-start.14) | collective-permute-done | bytes 688160 | tf_op jit(solution)/shard_map/ppermute | solution.py:423
  110.1 2.7 %mix.6 = (bf16[672,512]{1,0:T(8,128)(2,1)}, bf16[672,512]{1,0:T(8,128)(2,1)}, bf16[672,512]{1,0:T(8,128)(2,1)}) custom-call(bf16[4,672,512]{2,1,0:T(8,128)(2,1)} %bitcast.34, bf16[672,512]{1,0:T(8,128)(2,1)} %collective-permute-done.14.refs_1_, bf16[4,128,2688]{2,1,0:T(8,128)(2,1)} %token_terms.4.refs_2_.refs_0_, ...), custom_call_target="tpu_custom_call" | custom-call | flops 1 | bytes 1 | tf_op jit(solution)/shard_map/mix/pallas_call | solution.py:338
  112.8 5.4 %collective-permute-start.15 = (bf16[672,512]{1,0:T(8,128)(2,1)}, bf16[672,512]{1,0:T(8,128)(2,1)}, u32[]{:S(2)}, u32[]{:S(2)}) collective-permute-start(bf16[672,512]{1,0:T(8,128)(2,1)} %get-tuple-element.39.refs_9_), channel_id=1, source_target_pairs={{0,8},{24,16},{1,9},{25,17},{2,10},{26,18},{3,11},{27,19},{4,12},{... | collective-permute-start | bytes 2064392 | tf_op jit(solution)/shard_map/ppermute | solution.py:423
  118.2 1.6 collective-permute-start.16
  119.8 2.6 %collective-permute-start.17 = (bf16[672,512]{1,0:T(8,128)(2,1)}, bf16[672,512]{1,0:T(8,128)(2,1)}, u32[]{:S(2)}, u32[]{:S(2)}) collective-permute-start(bf16[672,512]{1,0:T(8,128)(2,1)} %get-tuple-element.41.refs_11_), channel_id=1, source_target_pairs={{0,8},{24,16},{1,9},{25,17},{2,10},{26,18},{3,11},{27,19},{4,12},{... | collective-permute-start | bytes 2064392 | tf_op jit(solution)/shard_map/ppermute | solution.py:423
  122.4 24.1 %heads.3 = (bf16[1024,256]{1,0:T(8,128)(2,1)}, bf16[1024,512]{1,0:T(8,128)(2,1)}, bf16[2688,512]{1,0:T(8,128)(2,1)}, bf16[2688,512]{1,0:T(8,128)(2,1)}) custom-call(s32[1,4]{1,0:T(1,128)} %lengths_ref.3, f32[1,128]{1,0:T(1,128)} %bitcast.47, f32[1,128]{1,0:T(1,128)} %bitcast.49, bf16[672,512]{1,0:T(8,128)(2,1)} %pad_maximum_fusion.1.refs_0_, ...), custom_call_target="tpu_custom_call" | custom-call | flops 8858370048 | bytes 17956864 | tf_op jit(solution)/shard_map/heads/pallas_call | solution.py:200
  146.5 2.2 mix.7
  149.7 6.0 %token_terms.5 = (bf16[128,2688]{1,0:T(8,128)(2,1)}, bf16[128,2688]{1,0:T(8,128)(2,1)}, bf16[128,2688]{1,0:T(8,128)(2,1)}, bf16[128,2688]{1,0:T(8,128)(2,1)}) custom-call(s32[1]{0:T(128)} %bitcast.7.side_ref, bf16[4,2,128,512]{3,2,1,0:T(8,128)(2,1)} %bitcast.41, bf16[2688,512]{1,0:T(8,128)(2,1)} %get-tuple-element.46.weight_ref, ...), custom_call_target="tpu_custom_call" | custom-call | flops 524288 | bytes 524288 | tf_op jit(solution)/shard_map/token_terms/pallas_call | solution.py:275
  156.8 4.9 %token_terms.6.refs_2_.refs_0_ = bf16[4,128,2688]{2,1,0:T(8,128)(2,1)} custom-call(s32[1]{0:T(128)} %bitcast.10.side_ref, bf16[4,2,128,512]{3,2,1,0:T(8,128)(2,1)} %bitcast.38, bf16[2688,512]{1,0:T(8,128)(2,1)} %get-tuple-element.38.weight_ref, bf16[128,2688]{1,0:T(8,128)(2,1)} %get-tuple-element.48.refs_0_, bf16[128,2688]{1,0:T(8,128)(2,1)} %get-tuple-element.49.refs_1_, ...), custom_call_target="tpu_custom_call" | custom-call | flops 524288 | bytes 524288 | tf_op jit(solution)/shard_map/token_terms/pallas_call | solution.py:275
  162.8 2.2 mix.8
  165.0 4.1 %collective-permute-start.19 = (bf16[672,512]{1,0:T(8,128)(2,1)}, bf16[672,512]{1,0:T(8,128)(2,1)}, u32[]{:S(2)}, u32[]{:S(2)}) collective-permute-start(bf16[672,512]{1,0:T(8,128)(2,1)} %get-tuple-element.52.refs_5_), channel_id=1, source_target_pairs={{0,8},{24,16},{1,9},{25,17},{2,10},{26,18},{3,11},{27,19},{4,12},{... | collective-permute-start | bytes 2064392 | tf_op jit(solution)/shard_map/ppermute | solution.py:423
  170.6 6.6 %token_terms.7.refs_3_ = bf16[4,128,2688]{2,1,0:T(8,128)(2,1)} custom-call(s32[1]{0:T(128)} %bitcast.10.side_ref, bf16[4,2,128,512]{3,2,1,0:T(8,128)(2,1)} %bitcast.42, bf16[2688,512]{1,0:T(8,128)(2,1)} %get-tuple-element.46.weight_ref, bf16[4,128,2688]{2,1,0:T(8,128)(2,1)} %token_terms.6.refs_2_.refs_0_, bf16[128,2688]{1,0:T(8,128)(2,1)} %collective-permute-done.21.refs_1_, ...), custom_call_target="tpu_custom_call" | custom-call | flops 524288 | bytes 524288 | tf_op jit(solution)/shard_map/token_terms/pallas_call | solution.py:275
  177.2 3.0 %dynamic-slice_bitcast_fusion.2 = (bf16[128,2688]{1,0:T(8,128)(2,1)}, bf16[128,2688]{1,0:T(8,128)(2,1)}, bf16[128,2688]{1,0:T(8,128)(2,1)}) fusion(bf16[4,128,2688]{2,1,0:T(8,128)(2,1)} %token_terms.7.refs_3_, s32[]{:T(128)S(6)} %select_n.19, s32[]{:T(128)S(6)} %select_n.21, s32[]{:T(128)S(6)} %select_n.20), kind=kLoop, calls=%fused_computation.10 | loop fusion | bytes 4128780 | tf_op jit(solution)/shard_map/jit(dynamic_index_in_dim)/squeeze | solution.py:588
  184.7 2.2 mix.9
  187.0 3.9 %all-to-all-start = ((bf16[8,128,512]{2,1,0:T(8,128)(2,1)}), bf16[8,128,512]{2,1,0:T(8,128)(2,1)S(1)}, u32[]{:S(2)}, u32[]{:S(2)}) async-start(bf16[8,128,512]{2,1,0:T(8,128)(2,1)} %bitcast.39), calls=%async_computation | async-start | bytes 2097152 | tf_op jit(solution)/shard_map/all_to_all | solution.py:593
  192.4 3.8 %collective-permute-start.29 = (bf16[672,512]{1,0:T(8,128)(2,1)S(1)}, bf16[672,512]{1,0:T(8,128)(2,1)}, u32[]{:S(2)}, u32[]{:S(2)}) collective-permute-start(bf16[672,512]{1,0:T(8,128)(2,1)S(1)} %copy-done.8), channel_id=1, source_target_pairs={{0,8},{8,0},{16,24},{24,16},{1,9},{9,1},{17,25},{25,17},{2,10},{10... | collective-permute-start | bytes 2064392 | tf_op jit(solution)/shard_map/ppermute | solution.py:423
  196.2 2.6 %collective-permute-done.25 = bf16[128,2688]{1,0:T(8,128)(2,1)} collective-permute-done((bf16[128,2688]{1,0:T(8,128)(2,1)}, bf16[128,2688]{1,0:T(8,128)(2,1)}, u32[]{:S(2)}, u32[]{:S(2)}) %collective-permute-start.25) | collective-permute-done | bytes 688160 | tf_op jit(solution)/shard_map/ppermute | solution.py:589
  200.4 16.1 %collective-permute-done.26 = bf16[128,2688]{1,0:T(8,128)(2,1)} collective-permute-done((bf16[128,2688]{1,0:T(8,128)(2,1)}, bf16[128,2688]{1,0:T(8,128)(2,1)}, u32[]{:S(2)}, u32[]{:S(2)}) %collective-permute-start.26) | collective-permute-done | bytes 688160 | tf_op jit(solution)/shard_map/ppermute | solution.py:589
  216.5 2.9 %fusion.2 = bf16[128,2688]{1,0:T(8,128)(2,1)} fusion(bf16[128,2688]{1,0:T(8,128)(2,1)} %collective-permute-done.27, bf16[128,2688]{1,0:T(8,128)(2,1)} %collective-permute-done.26, bf16[128,2688]{1,0:T(8,128)(2,1)} %collective-permute-done.25, bf16[4,128,2688]{2,1,0:T(8,128)(2,1)} %token_terms.7.refs_3_, s32[]{:T(128)S(6)} %select_n.18), kind=kLoop, calls=%fused_computation.3 | loop fusion | flops 2752512 | bytes 3440644 | tf_op jit(solution)/shard_map/convert_element_type | solution.py:606
  219.4 4.5 %all-to-all-done = bf16[8,128,512]{2,1,0:T(8,128)(2,1)S(1)} async-done(((bf16[8,128,512]{2,1,0:T(8,128)(2,1)}), bf16[8,128,512]{2,1,0:T(8,128)(2,1)S(1)}, u32[]{:S(2)}, u32[]{:S(2)}) %all-to-all-start) | async-done | bytes 1048608 | tf_op jit(solution)/shard_map/all_to_all | solution.py:593
  225.0 3.9 %total_terms.1 = (f32[672,512]{1,0:T(8,128)}, f32[672,256]{1,0:T(8,128)}, f32[672,256]{1,0:T(8,128)}) custom-call(bf16[4,672,512]{2,1,0:T(8,128)(2,1)} %bitcast.36, bf16[672,512]{1,0:T(8,128)(2,1)} %collective-permute-done.17.refs_4_.refs_1_, bf16[672,512]{1,0:T(8,128)(2,1)} %collective-permute-done.18.refs_1_.refs_2_, ...), custom_call_target="tpu_custom_call" | custom-call | flops 1 | bytes 1 | tf_op jit(solution)/shard_map/total_terms/pallas_call | solution.py:390
  (103 shorter events, 30.6 us)
Async XLA Ops:
  7.2 59.6 %all-gather.2.cloned.1.call-start = ((), (), s32[]{:S(2)}) async-start(), calls=%async_computation.1 | async-start | bytes 6193152 | tf_op jit(solution)/shard_map/all_gather | solution.py:497
  9.2 12.0 %collective-permute-start.5 = (bf16[672,256]{1,0:T(8,128)(2,1)S(1)}, bf16[672,256]{1,0:T(8,128)(2,1)S(1)}, u32[]{:S(2)}, u32[]{:S(2)}) collective-permute-start(bf16[672,256]{1,0:T(8,128)(2,1)S(1)} %pad_maximum_fusion.4.refs_6_), channel_id=1, source_target_pairs={{0,8},{8,0},{16,24},{24,16},{1,9},{9,1},{17,25},{25,17},{2,10},{10... | collective-permute-start | bytes 1032200 | tf_op jit(solution)/shard_map/ppermute | solution.py:423
  12.3 19.4 %collective-permute-start.6 = (bf16[672,256]{1,0:T(8,128)(2,1)S(1)}, bf16[672,256]{1,0:T(8,128)(2,1)S(1)}, u32[]{:S(2)}, u32[]{:S(2)}) collective-permute-start(bf16[672,256]{1,0:T(8,128)(2,1)S(1)} %pad_maximum_fusion.4.refs_6_), channel_id=1, source_target_pairs={{8,16},{16,8},{9,17},{17,9},{10,18},{18,10},{11,19},{19,11},{12,20... | collective-permute-start | bytes 1032200 | tf_op jit(solution)/shard_map/ppermute | solution.py:423
  13.0 14.7 %collective-permute-start = (bf16[672,256]{1,0:T(8,128)(2,1)S(1)}, bf16[672,256]{1,0:T(8,128)(2,1)S(1)}, u32[]{:S(2)}, u32[]{:S(2)}) collective-permute-start(bf16[672,256]{1,0:T(8,128)(2,1)S(1)} %get-tuple-element.66.refs_0_), channel_id=1, source_target_pairs={{0,8},{8,0},{16,24},{24,16},{1,9},{9,1},{17,25},{25,17},{2,10},{10... | collective-permute-start | bytes 1032200 | tf_op jit(solution)/shard_map/ppermute | solution.py:423
  17.5 15.5 %collective-permute-start.1 = (bf16[672,256]{1,0:T(8,128)(2,1)S(1)}, bf16[672,256]{1,0:T(8,128)(2,1)S(1)}, u32[]{:S(2)}, u32[]{:S(2)}) collective-permute-start(bf16[672,256]{1,0:T(8,128)(2,1)S(1)} %get-tuple-element.66.refs_0_), channel_id=1, source_target_pairs={{8,16},{16,8},{9,17},{17,9},{10,18},{18,10},{11,19},{19,11},{12,20... | collective-permute-start | bytes 1032200 | tf_op jit(solution)/shard_map/ppermute | solution.py:423
  21.2 13.1 %collective-permute-start.7 = (bf16[672,256]{1,0:T(8,128)(2,1)S(1)}, bf16[672,256]{1,0:T(8,128)(2,1)S(1)}, u32[]{:S(2)}, u32[]{:S(2)}) collective-permute-start(bf16[672,256]{1,0:T(8,128)(2,1)S(1)} %collective-permute-done.5.refs_7_), channel_id=1, source_target_pairs={{8,16},{16,8},{9,17},{17,9},{10,18},{18,10},{11,19},{19,11},{12,20... | collective-permute-start | bytes 1032200 | tf_op jit(solution)/shard_map/ppermute | solution.py:423
  31.7 35.1 %collective-permute-start.8 = (bf16[672,256]{1,0:T(8,128)(2,1)S(1)}, bf16[672,256]{1,0:T(8,128)(2,1)S(1)}, u32[]{:S(2)}, u32[]{:S(2)}) collective-permute-start(bf16[672,256]{1,0:T(8,128)(2,1)S(1)} %collective-permute-done.6.refs_8_), channel_id=1, source_target_pairs={{8,0},{16,24},{9,1},{17,25},{10,2},{18,26},{11,3},{19,27},{12,4},{... | collective-permute-start | bytes 1032200 | tf_op jit(solution)/shard_map/ppermute | solution.py:423
  33.0 20.8 %collective-permute-start.3 = (bf16[672,256]{1,0:T(8,128)(2,1)S(1)}, bf16[672,256]{1,0:T(8,128)(2,1)S(1)}, u32[]{:S(2)}, u32[]{:S(2)}) collective-permute-start(bf16[672,256]{1,0:T(8,128)(2,1)S(1)} %collective-permute-done.1.refs_2_), channel_id=1, source_target_pairs={{8,0},{16,24},{9,1},{17,25},{10,2},{18,26},{11,3},{19,27},{12,4},{... | collective-permute-start | bytes 1032200 | tf_op jit(solution)/shard_map/ppermute | solution.py:423
  34.3 32.5 %collective-permute-start.9 = (bf16[672,256]{1,0:T(8,128)(2,1)S(1)}, bf16[672,256]{1,0:T(8,128)(2,1)S(1)}, u32[]{:S(2)}, u32[]{:S(2)}) collective-permute-start(bf16[672,256]{1,0:T(8,128)(2,1)S(1)} %collective-permute-done.7.refs_9_), channel_id=1, source_target_pairs={{8,0},{16,24},{9,1},{17,25},{10,2},{18,26},{11,3},{19,27},{12,4},{... | collective-permute-start | bytes 1032200 | tf_op jit(solution)/shard_map/ppermute | solution.py:423
  35.7 31.1 %collective-permute-start.4 = (bf16[672,256]{1,0:T(8,128)(2,1)S(1)}, bf16[672,256]{1,0:T(8,128)(2,1)S(1)}, u32[]{:S(2)}, u32[]{:S(2)}) collective-permute-start(bf16[672,256]{1,0:T(8,128)(2,1)S(1)} %collective-permute-done.2.refs_3_), channel_id=1, source_target_pairs={{8,0},{16,24},{9,1},{17,25},{10,2},{18,26},{11,3},{19,27},{12,4},{... | collective-permute-start | bytes 1032200 | tf_op jit(solution)/shard_map/ppermute | solution.py:423
  53.9 44.1 %collective-permute-start.12 = (bf16[672,512]{1,0:T(8,128)(2,1)}, bf16[672,512]{1,0:T(8,128)(2,1)}, u32[]{:S(2)}, u32[]{:S(2)}) collective-permute-start(bf16[672,512]{1,0:T(8,128)(2,1)} %pad_maximum_fusion.1.refs_0_), channel_id=1, source_target_pairs={{0,16},{8,24},{16,0},{24,8},{1,17},{9,25},{17,1},{25,9},{2,18},{10... | collective-permute-start | bytes 2064392 | tf_op jit(solution)/shard_map/ppermute | solution.py:423
  53.9 50.3 %collective-permute-start.11 = (bf16[672,512]{1,0:T(8,128)(2,1)}, bf16[672,512]{1,0:T(8,128)(2,1)}, u32[]{:S(2)}, u32[]{:S(2)}) collective-permute-start(bf16[672,512]{1,0:T(8,128)(2,1)} %pad_maximum_fusion.1.refs_0_), channel_id=1, source_target_pairs={{8,16},{16,8},{9,17},{17,9},{10,18},{18,10},{11,19},{19,11},{12,20... | collective-permute-start | bytes 2064392 | tf_op jit(solution)/shard_map/ppermute | solution.py:423
  66.7 37.4 %collective-permute-start.10 = (bf16[672,512]{1,0:T(8,128)(2,1)}, bf16[672,512]{1,0:T(8,128)(2,1)}, u32[]{:S(2)}, u32[]{:S(2)}) collective-permute-start(bf16[672,512]{1,0:T(8,128)(2,1)} %pad_maximum_fusion.1.refs_0_), channel_id=1, source_target_pairs={{0,8},{8,0},{16,24},{24,16},{1,9},{9,1},{17,25},{25,17},{2,10},{10... | collective-permute-start | bytes 2064392 | tf_op jit(solution)/shard_map/ppermute | solution.py:423
  93.9 16.3 %collective-permute-start.14 = (bf16[672,512]{1,0:T(8,128)(2,1)}, bf16[672,512]{1,0:T(8,128)(2,1)}, u32[]{:S(2)}, u32[]{:S(2)}) collective-permute-start(bf16[672,512]{1,0:T(8,128)(2,1)} %mix.5.refs_0_), channel_id=1, source_target_pairs={{0,8},{24,16},{1,9},{25,17},{2,10},{26,18},{3,11},{27,19},{4,12},{... | collective-permute-start | bytes 2064392 | tf_op jit(solution)/shard_map/ppermute | solution.py:423
  98.0 24.4 %collective-permute-start.13 = (bf16[672,512]{1,0:T(8,128)(2,1)}, bf16[672,512]{1,0:T(8,128)(2,1)}, u32[]{:S(2)}, u32[]{:S(2)}) collective-permute-start(bf16[672,512]{1,0:T(8,128)(2,1)} %collective-permute-done.12.refs_1_.refs_3_), channel_id=1, source_target_pairs={{8,0},{16,24},{9,1},{17,25},{10,2},{18,26},{11,3},{19,27},{12,4},{... | collective-permute-start | bytes 2064392 | tf_op jit(solution)/shard_map/ppermute | solution.py:423
  112.8 33.6 %collective-permute-start.15 = (bf16[672,512]{1,0:T(8,128)(2,1)}, bf16[672,512]{1,0:T(8,128)(2,1)}, u32[]{:S(2)}, u32[]{:S(2)}) collective-permute-start(bf16[672,512]{1,0:T(8,128)(2,1)} %get-tuple-element.39.refs_9_), channel_id=1, source_target_pairs={{0,8},{24,16},{1,9},{25,17},{2,10},{26,18},{3,11},{27,19},{4,12},{... | collective-permute-start | bytes 2064392 | tf_op jit(solution)/shard_map/ppermute | solution.py:423
  118.2 28.2 %collective-permute-start.16 = (bf16[672,512]{1,0:T(8,128)(2,1)}, bf16[672,512]{1,0:T(8,128)(2,1)}, u32[]{:S(2)}, u32[]{:S(2)}) collective-permute-start(bf16[672,512]{1,0:T(8,128)(2,1)} %get-tuple-element.40.refs_10_), channel_id=1, source_target_pairs={{8,16},{16,8},{9,17},{17,9},{10,18},{18,10},{11,19},{19,11},{12,20... | collective-permute-start | bytes 2064392 | tf_op jit(solution)/shard_map/ppermute | solution.py:423
  119.8 26.7 %collective-permute-start.17 = (bf16[672,512]{1,0:T(8,128)(2,1)}, bf16[672,512]{1,0:T(8,128)(2,1)}, u32[]{:S(2)}, u32[]{:S(2)}) collective-permute-start(bf16[672,512]{1,0:T(8,128)(2,1)} %get-tuple-element.41.refs_11_), channel_id=1, source_target_pairs={{0,8},{24,16},{1,9},{25,17},{2,10},{26,18},{3,11},{27,19},{4,12},{... | collective-permute-start | bytes 2064392 | tf_op jit(solution)/shard_map/ppermute | solution.py:423
  148.7 14.1 %collective-permute-start.18 = (bf16[672,512]{1,0:T(8,128)(2,1)}, bf16[672,512]{1,0:T(8,128)(2,1)}, u32[]{:S(2)}, u32[]{:S(2)}) collective-permute-start(bf16[672,512]{1,0:T(8,128)(2,1)} %get-tuple-element.44.refs_1_), channel_id=1, source_target_pairs={{0,8},{8,0},{16,24},{24,16},{1,9},{9,1},{17,25},{25,17},{2,10},{10... | collective-permute-start | bytes 2064392 | tf_op jit(solution)/shard_map/ppermute | solution.py:423
  155.8 13.3 %collective-permute-start.21 = (bf16[128,2688]{1,0:T(8,128)(2,1)}, bf16[128,2688]{1,0:T(8,128)(2,1)}, u32[]{:S(2)}, u32[]{:S(2)}) collective-permute-start(bf16[128,2688]{1,0:T(8,128)(2,1)} %get-tuple-element.48.refs_0_), channel_id=1, source_target_pairs={{0,1},{1,0},{2,3},{3,2},{4,5},{5,4},{6,7},{7,6},{8,9},{9,8},{10,11... | collective-permute-start | bytes 2064392 | tf_op jit(solution)/shard_map/ppermute | solution.py:579
  155.8 14.8 %collective-permute-start.22 = (bf16[128,2688]{1,0:T(8,128)(2,1)}, bf16[128,2688]{1,0:T(8,128)(2,1)}, u32[]{:S(2)}, u32[]{:S(2)}) collective-permute-start(bf16[128,2688]{1,0:T(8,128)(2,1)} %get-tuple-element.49.refs_1_), channel_id=1, source_target_pairs={{0,1},{1,0},{2,3},{3,2},{4,5},{5,4},{6,7},{7,6},{8,9},{9,8},{10,11... | collective-permute-start | bytes 2064392 | tf_op jit(solution)/shard_map/ppermute | solution.py:579
  156.3 14.3 %collective-permute-start.23 = (bf16[128,2688]{1,0:T(8,128)(2,1)}, bf16[128,2688]{1,0:T(8,128)(2,1)}, u32[]{:S(2)}, u32[]{:S(2)}) collective-permute-start(bf16[128,2688]{1,0:T(8,128)(2,1)} %get-tuple-element.50.refs_2_), channel_id=1, source_target_pairs={{0,1},{1,0},{2,3},{3,2},{4,5},{5,4},{6,7},{7,6},{8,9},{9,8},{10,11... | collective-permute-start | bytes 2064392 | tf_op jit(solution)/shard_map/ppermute | solution.py:579
  156.3 14.3 %collective-permute-start.24 = (bf16[128,2688]{1,0:T(8,128)(2,1)}, bf16[128,2688]{1,0:T(8,128)(2,1)}, u32[]{:S(2)}, u32[]{:S(2)}) collective-permute-start(bf16[128,2688]{1,0:T(8,128)(2,1)} %get-tuple-element.51.refs_3_), channel_id=1, source_target_pairs={{0,1},{1,0},{2,3},{3,2},{4,5},{5,4},{6,7},{7,6},{8,9},{9,8},{10,11... | collective-permute-start | bytes 2064392 | tf_op jit(solution)/shard_map/ppermute | solution.py:579
  165.0 19.7 %collective-permute-start.19 = (bf16[672,512]{1,0:T(8,128)(2,1)}, bf16[672,512]{1,0:T(8,128)(2,1)}, u32[]{:S(2)}, u32[]{:S(2)}) collective-permute-start(bf16[672,512]{1,0:T(8,128)(2,1)} %get-tuple-element.52.refs_5_), channel_id=1, source_target_pairs={{0,8},{24,16},{1,9},{25,17},{2,10},{26,18},{3,11},{27,19},{4,12},{... | collective-permute-start | bytes 2064392 | tf_op jit(solution)/shard_map/ppermute | solution.py:423
  169.1 15.6 %collective-permute-start.20 = (bf16[672,512]{1,0:T(8,128)(2,1)}, bf16[672,512]{1,0:T(8,128)(2,1)}, u32[]{:S(2)}, u32[]{:S(2)}) collective-permute-start(bf16[672,512]{1,0:T(8,128)(2,1)} %get-tuple-element.53.refs_6_), channel_id=1, source_target_pairs={{8,16},{16,8},{9,17},{17,9},{10,18},{18,10},{11,19},{19,11},{12,20... | collective-permute-start | bytes 2064392 | tf_op jit(solution)/shard_map/ppermute | solution.py:423
  180.2 18.7 %collective-permute-start.25 = (bf16[128,2688]{1,0:T(8,128)(2,1)}, bf16[128,2688]{1,0:T(8,128)(2,1)}, u32[]{:S(2)}, u32[]{:S(2)}) collective-permute-start(bf16[128,2688]{1,0:T(8,128)(2,1)} %get-tuple-element.61), channel_id=1, source_target_pairs={{0,2},{1,3},{2,0},{3,1},{4,6},{5,7},{6,4},{7,5},{8,10},{9,11},{10,... | collective-permute-start | bytes 2064392 | tf_op jit(solution)/shard_map/ppermute | solution.py:589
  181.6 34.8 %collective-permute-start.26 = (bf16[128,2688]{1,0:T(8,128)(2,1)}, bf16[128,2688]{1,0:T(8,128)(2,1)}, u32[]{:S(2)}, u32[]{:S(2)}) collective-permute-start(bf16[128,2688]{1,0:T(8,128)(2,1)} %get-tuple-element.63), channel_id=1, source_target_pairs={{0,4},{1,5},{2,6},{3,7},{4,0},{5,1},{6,2},{7,3},{8,12},{9,13},{10,... | collective-permute-start | bytes 2064392 | tf_op jit(solution)/shard_map/ppermute | solution.py:589
  183.2 33.3 %collective-permute-start.27 = (bf16[128,2688]{1,0:T(8,128)(2,1)}, bf16[128,2688]{1,0:T(8,128)(2,1)}, u32[]{:S(2)}, u32[]{:S(2)}) collective-permute-start(bf16[128,2688]{1,0:T(8,128)(2,1)} %get-tuple-element.62), channel_id=1, source_target_pairs={{0,6},{1,7},{2,4},{3,5},{4,2},{5,3},{6,0},{7,1},{8,14},{9,15},{10,... | collective-permute-start | bytes 2064392 | tf_op jit(solution)/shard_map/ppermute | solution.py:589
  187.0 37.0 %all-to-all-start = ((bf16[8,128,512]{2,1,0:T(8,128)(2,1)}), bf16[8,128,512]{2,1,0:T(8,128)(2,1)S(1)}, u32[]{:S(2)}, u32[]{:S(2)}) async-start(bf16[8,128,512]{2,1,0:T(8,128)(2,1)} %bitcast.39), calls=%async_computation | async-start | bytes 2097152 | tf_op jit(solution)/shard_map/all_to_all | solution.py:593
  190.8 34.2 %collective-permute-start.28 = (bf16[672,512]{1,0:T(8,128)(2,1)S(1)}, bf16[672,512]{1,0:T(8,128)(2,1)}, u32[]{:S(2)}, u32[]{:S(2)}) collective-permute-start(bf16[672,512]{1,0:T(8,128)(2,1)S(1)} %copy-done.2), channel_id=1, source_target_pairs={{8,16},{16,8},{9,17},{17,9},{10,18},{18,10},{11,19},{19,11},{12,20... | collective-permute-start | bytes 2064392 | tf_op jit(solution)/shard_map/ppermute | solution.py:423
  192.4 32.7 %collective-permute-start.29 = (bf16[672,512]{1,0:T(8,128)(2,1)S(1)}, bf16[672,512]{1,0:T(8,128)(2,1)}, u32[]{:S(2)}, u32[]{:S(2)}) collective-permute-start(bf16[672,512]{1,0:T(8,128)(2,1)S(1)} %copy-done.8), channel_id=1, source_target_pairs={{0,8},{8,0},{16,24},{24,16},{1,9},{9,1},{17,25},{25,17},{2,10},{10... | collective-permute-start | bytes 2064392 | tf_op jit(solution)/shard_map/ppermute | solution.py:423
  198.8 26.2 %collective-permute-start.30 = (bf16[672,512]{1,0:T(8,128)(2,1)S(1)}, bf16[672,512]{1,0:T(8,128)(2,1)}, u32[]{:S(2)}, u32[]{:S(2)}) collective-permute-start(bf16[672,512]{1,0:T(8,128)(2,1)S(1)} %copy-done.7), channel_id=1, source_target_pairs={{8,16},{16,8},{9,17},{17,9},{10,18},{18,10},{11,19},{19,11},{12,20... | collective-permute-start | bytes 2064392 | tf_op jit(solution)/shard_map/ppermute | solution.py:423
  (21 other events, 242.1 us)
Sparse Core Ops, SparseCore 0:
  9.9 44.9 all-gather.1
